TPU v7x, 32 devices: a whole 2x2x4 slice. The times are simulated.
32 devices in a mesh: gx: 2 (over x), yz: 16 (over z, y, core).
Axes of the slice: x: 2, y: 2, z: 4, core: 2. Of those that a mesh axis runs over, the one named last changes fastest.
Arguments:
- old_coeff: bfloat16 [8192, 512], P(('gx', 'yz')), may hold values from -6 to 6
- basis_old: bfloat16 [8, 64, 64], replicated, may hold values from -0.75 to 0.75
- basis_new: bfloat16 [8, 64, 64], replicated, may hold values from -0.75 to 0.75
- quad_weight: float32 [8, 64], replicated, may hold values from 0.3 to 3
- tet_zone: int32 [65536], P(('gx', 'yz')), may hold values from 0 to 255
- tet_table: int32 [65536], P(('gx', 'yz')), may hold values from 0 to 7
- tet_volume: float32 [65536], P(('gx', 'yz')), may hold values from 0.1 to 1
- tet_dest: int32 [65536], P(('gx', 'yz')), may hold values from 0 to 415, as said below
- recv_list: int32 [32, 160], P(('gx', 'yz')), may hold values from 0 to 255
- inv_mass: bfloat16 [8192, 4096], P(('gx', 'yz')), may hold values from -0.75 to 0.75
Outputs:
- new_coeff: float32 [8192, 512], P(('gx', 'yz'))
Inputs may be any that keep to these rules, and one draw needn't show every extreme that they name: `tet_dest`: A value below 256 names an own new zone; 256 + k * 16 + s names slot s of partner k.
All inputs are finite; a program needn't handle non-finite values.
Results may differ from a plain program's by a relative error of at most 0.0042.
Values may be sent and summed in bfloat16 or wider, within the bound.
A program may use at most 64 MiB of HBM per device.

v0:
```python
import jax
import jax.numpy as jnp
from jax import lax
from jax.sharding import PartitionSpec as P


def extended_2(block, sides, width):
    for axis, dim in sides:
        count = lax.axis_size(axis)
        forward = [(i, i + 1) for i in range(count - 1)]
        forward.append((count - 1, 0))
        backward = [(target, source) for source, target in forward]
        low = lax.ppermute(
            lax.slice_in_dim(block, block.shape[dim] - width, None, axis=dim), axis, forward
        )
        high = lax.ppermute(lax.slice_in_dim(block, 0, width, axis=dim), axis, backward)
        block = jnp.concatenate([low, block, high], axis=dim)
    return block


def passed_along(block, axis, distance):
    devices = range(lax.axis_size(axis))
    route = [((i - distance) % len(devices), i) for i in devices]
    return lax.ppermute(block, axis, route)


def on_device(
    old_coeff,
    basis_old,
    basis_new,
    quad_weight,
    tet_zone,
    tet_table,
    tet_volume,
    tet_dest,
    recv_list,
    inv_mass,
):
    zone_count = old_coeff.shape[0]
    row_width = old_coeff.shape[1]
    tables = basis_old.shape[0]
    basis_size = basis_old.shape[2]
    field_count = row_width // basis_size
    tet_count = tet_zone.shape[0]
    slot_total = recv_list.shape[1]
    partner_count = 10
    slot_cap = slot_total // partner_count
    row_count = zone_count + slot_total
    block_rows = min(512, tet_count)
    block_count = tet_count // block_rows

    def quad_block(partial_value, pieces):
        zone_blk, table_blk, volume_blk, dest_blk = pieces
        picked = jnp.take(old_coeff, zone_blk, axis=0).reshape(block_rows, basis_size, field_count)
        values = jnp.einsum("tqi,bif->btqf", basis_old, picked, preferred_element_type=jnp.float32)
        selector = (table_blk[:, None] == jnp.arange(tables, dtype=jnp.int32)[None, :]).astype(
            jnp.float32
        )
        scaling = selector[:, :, None] * quad_weight[None, :, :] * volume_blk[:, None, None]
        weighted = jnp.sum(scaling[:, :, :, None] * values, axis=1).astype(jnp.bfloat16)
        spread = selector.astype(jnp.bfloat16)[:, :, None, None] * weighted[:, None, :, :]
        moment = jnp.einsum("btqf,tqj->bjf", spread, basis_new, preferred_element_type=jnp.float32)
        partial_value = partial_value + jax.ops.segment_sum(
            moment.reshape(block_rows, row_width), dest_blk, num_segments=row_count
        )
        return (partial_value, None)

    pieces = (
        tet_zone.reshape(block_count, block_rows),
        tet_table.reshape(block_count, block_rows),
        tet_volume.reshape(block_count, block_rows),
        tet_dest.reshape(block_count, block_rows),
    )
    partial_value, _ = lax.scan(quad_block, jnp.zeros((row_count, row_width), jnp.float32), pieces)
    own_part = partial_value[:zone_count]
    outgoing = (
        partial_value[zone_count:].astype(jnp.bfloat16).reshape(partner_count, slot_cap, row_width)
    )
    lane_count = lax.axis_size("yz")
    face_side = 1 << (lane_count.bit_length() - 1) // 2
    going_down = jnp.stack([outgoing[1], outgoing[5], outgoing[6]], axis=0)
    going_up = jnp.stack([outgoing[0], outgoing[4], outgoing[7]], axis=0)
    stepped = extended_2(jnp.stack([going_down, going_up], axis=0), (("yz", 0),), 1)
    from_left = stepped[0]
    from_right = stepped[3]
    upward = jnp.stack([outgoing[2], from_left[1], from_right[2]], axis=0)
    downward = jnp.stack([outgoing[3], from_left[2], from_right[1]], axis=0)
    came_up = passed_along(upward, "yz", face_side)
    came_down = passed_along(downward, "yz", lane_count - face_side)
    face_rows = jnp.stack(
        [
            from_left[0],
            from_right[0],
            came_up[0],
            came_down[0],
            came_up[1],
            came_down[2],
            came_up[2],
            came_down[1],
        ],
        axis=0,
    )
    sweep_rows = jnp.stack([outgoing[9], outgoing[8]], axis=0)
    extended = extended_2(sweep_rows, (("gx", 0),), 1)
    received = jnp.concatenate([face_rows, extended[0:1], extended[3:4]], axis=0).reshape(
        slot_total, row_width
    )
    gathered = own_part + jax.ops.segment_sum(
        received.astype(jnp.float32), recv_list[0], num_segments=zone_count
    )
    rounded = gathered.astype(jnp.bfloat16).reshape(zone_count, basis_size, field_count)
    inverse = inv_mass.reshape(zone_count, basis_size, basis_size)
    result = jnp.einsum("zjk,zkf->zjf", inverse, rounded, preferred_element_type=jnp.float32)
    return result.reshape(zone_count, row_width)


def solution(mesh):
    placed = (
        P(("gx", "yz"), None),
        P(),
        P(),
        P(),
        P(("gx", "yz")),
        P(("gx", "yz")),
        P(("gx", "yz")),
        P(("gx", "yz")),
        P(("gx", "yz"), None),
        P(("gx", "yz"), None),
    )
    return jax.shard_map(
        on_device, mesh=mesh, in_specs=placed, out_specs=P(("gx", "yz"), None), check_vma=False
    )
```

profile of v0, /device:TPU:0, one launch (start us, length us, event | category | flops | bytes accessed | tf_op | source)
XLA Modules:
  0.0 82.8 jit_solution(4906633874098280122)
XLA Ops:
  2.8 1.0 %copy.29 = bf16[8,64,64]{1,2,0:T(8,128)(2,1)S(1)} copy(bf16[8,64,64]{2,1,0:T(8,128)(2,1)} %param.14) | data formatting | bytes 131072 | tf_op jit(solution)/shard_map/while | solution.py:74
  4.0 42.6 %while.10 = (s32[]{:T(128)}, f32[416,512]{1,0:T(8,128)S(1)}, s32[4,512]{1,0:T(4,128)S(1)}, s32[4,512]{1,0:T(4,128)S(1)}, f32[8,64]{1,0:T(8,128)}, /*index=5*/f32...) while((s32[]{:T(128)}, f32[416,512]{1,0:T(8,128)S(1)}, ...), condition=%wide.region_3.4_spmd, body=%wide.region_0.3_spmd.sunk | while | flops 550258176 | bytes 15692985 | solution.py:74
  4.1 3.0 %gather_fusion = bf16[512,512]{1,0:T(8,128)(2,1)S(1)} fusion(bf16[256,512]{1,0:T(8,128)(2,1)} %get-tuple-element.230, s32[1024]{0:T(1024)S(1)} %pad_clamp_fusion.2), kind=kCustom, calls=%fused_computation.clone.1 | custom fusion | bytes 1050624 | tf_op jit(solution)/shard_map/while/body/eval_jaxpr/jit(_take)/gather | solution.py:54
  7.5 1.3 %multiply_reduce_fusion.2 = bf16[512,8,64]{0,2,1:T(8,128)(2,1)S(1)} fusion(f32[512,8,64]{0,2,1:T(8,128)S(1)} %multiply_multiply_fusion.2, bf16[512,64,8,1]{0,2,1,3:T(8,128)(2,1)S(1)} %fusion.29, bf16[8,64,64]{2,1,0:T(8,128)(2,1)S(1)} %copy-done.1), kind=kOutput, calls=%fused_computation.3.clone.1 | convolution fusion | flops 272367616 | bytes 2162688 | tf_op jit(solution)/shard_map/while/body/eval_jaxpr/tqi,bif->btqf/dot_general | solution.py:55
  10.7 3.9 %scatter_fusion = f32[416,512]{1,0:T(8,128)S(1)} fusion(f32[416,512]{1,0:T(8,128)S(1)} %get-tuple-element.213, s32[512]{0:T(512)S(1)} %bitcast.110, f32[512,512]{1,0:T(8,128)S(1)} %copy.51), kind=kCustom, calls=%fused_computation.1.clone.1 | custom fusion | flops 262144 | bytes 3147776 | tf_op jit(solution)/shard_map/while/body/eval_jaxpr/scatter-add | solution.py:63
  14.7 3.0 %gather_fusion = bf16[512,512]{1,0:T(8,128)(2,1)S(1)} fusion(bf16[256,512]{1,0:T(8,128)(2,1)} %get-tuple-element.230, s32[1024]{0:T(1024)S(1)} %pad_clamp_fusion.2), kind=kCustom, calls=%fused_computation.clone.1 | custom fusion | bytes 1050624 | tf_op jit(solution)/shard_map/while/body/eval_jaxpr/jit(_take)/gather | solution.py:54
  18.2 1.3 %multiply_reduce_fusion.2 = bf16[512,8,64]{0,2,1:T(8,128)(2,1)S(1)} fusion(f32[512,8,64]{0,2,1:T(8,128)S(1)} %multiply_multiply_fusion.2, bf16[512,64,8,1]{0,2,1,3:T(8,128)(2,1)S(1)} %fusion.29, bf16[8,64,64]{2,1,0:T(8,128)(2,1)S(1)} %copy-done.1), kind=kOutput, calls=%fused_computation.3.clone.1 | convolution fusion | flops 272367616 | bytes 2162688 | tf_op jit(solution)/shard_map/while/body/eval_jaxpr/tqi,bif->btqf/dot_general | solution.py:55
  19.5 0.9 %fusion.30 = f32[512,64,8]{0,1,2:T(8,128)S(1)} fusion(bf16[512,64,8]{0,1,2:T(8,128)(2,1)S(1)} %bitcast.117, bf16[512,8]{0,1:T(8,128)(2,1)S(1)} %get-tuple-element.200, bf16[8,64,64]{1,2,0:T(8,128)(2,1)S(1)} %get-tuple-element.232), kind=kOutput, calls=%fused_computation.8.clone.1 | convolution fusion | flops 276824064 | bytes 1646592 | tf_op jit(solution)/shard_map/while/body/eval_jaxpr/btqf,tqj->bjf/dot_general | solution.py:62
  21.3 3.9 %scatter_fusion = f32[416,512]{1,0:T(8,128)S(1)} fusion(f32[416,512]{1,0:T(8,128)S(1)} %get-tuple-element.213, s32[512]{0:T(512)S(1)} %bitcast.110, f32[512,512]{1,0:T(8,128)S(1)} %copy.51), kind=kCustom, calls=%fused_computation.1.clone.1 | custom fusion | flops 262144 | bytes 3147776 | tf_op jit(solution)/shard_map/while/body/eval_jaxpr/scatter-add | solution.py:63
  25.4 3.0 %gather_fusion = bf16[512,512]{1,0:T(8,128)(2,1)S(1)} fusion(bf16[256,512]{1,0:T(8,128)(2,1)} %get-tuple-element.230, s32[1024]{0:T(1024)S(1)} %pad_clamp_fusion.2), kind=kCustom, calls=%fused_computation.clone.1 | custom fusion | bytes 1050624 | tf_op jit(solution)/shard_map/while/body/eval_jaxpr/jit(_take)/gather | solution.py:54
  28.8 1.3 %multiply_reduce_fusion.2 = bf16[512,8,64]{0,2,1:T(8,128)(2,1)S(1)} fusion(f32[512,8,64]{0,2,1:T(8,128)S(1)} %multiply_multiply_fusion.2, bf16[512,64,8,1]{0,2,1,3:T(8,128)(2,1)S(1)} %fusion.29, bf16[8,64,64]{2,1,0:T(8,128)(2,1)S(1)} %copy-done.1), kind=kOutput, calls=%fused_computation.3.clone.1 | convolution fusion | flops 272367616 | bytes 2162688 | tf_op jit(solution)/shard_map/while/body/eval_jaxpr/tqi,bif->btqf/dot_general | solution.py:55
  30.1 0.9 %fusion.30 = f32[512,64,8]{0,1,2:T(8,128)S(1)} fusion(bf16[512,64,8]{0,1,2:T(8,128)(2,1)S(1)} %bitcast.117, bf16[512,8]{0,1:T(8,128)(2,1)S(1)} %get-tuple-element.200, bf16[8,64,64]{1,2,0:T(8,128)(2,1)S(1)} %get-tuple-element.232), kind=kOutput, calls=%fused_computation.8.clone.1 | convolution fusion | flops 276824064 | bytes 1646592 | tf_op jit(solution)/shard_map/while/body/eval_jaxpr/btqf,tqj->bjf/dot_general | solution.py:62
  32.0 3.9 %scatter_fusion = f32[416,512]{1,0:T(8,128)S(1)} fusion(f32[416,512]{1,0:T(8,128)S(1)} %get-tuple-element.213, s32[512]{0:T(512)S(1)} %bitcast.110, f32[512,512]{1,0:T(8,128)S(1)} %copy.51), kind=kCustom, calls=%fused_computation.1.clone.1 | custom fusion | flops 262144 | bytes 3147776 | tf_op jit(solution)/shard_map/while/body/eval_jaxpr/scatter-add | solution.py:63
  36.0 3.0 %gather_fusion = bf16[512,512]{1,0:T(8,128)(2,1)S(1)} fusion(bf16[256,512]{1,0:T(8,128)(2,1)} %get-tuple-element.230, s32[1024]{0:T(1024)S(1)} %pad_clamp_fusion.2), kind=kCustom, calls=%fused_computation.clone.1 | custom fusion | bytes 1050624 | tf_op jit(solution)/shard_map/while/body/eval_jaxpr/jit(_take)/gather | solution.py:54
  39.5 1.3 %multiply_reduce_fusion.2 = bf16[512,8,64]{0,2,1:T(8,128)(2,1)S(1)} fusion(f32[512,8,64]{0,2,1:T(8,128)S(1)} %multiply_multiply_fusion.2, bf16[512,64,8,1]{0,2,1,3:T(8,128)(2,1)S(1)} %fusion.29, bf16[8,64,64]{2,1,0:T(8,128)(2,1)S(1)} %copy-done.1), kind=kOutput, calls=%fused_computation.3.clone.1 | convolution fusion | flops 272367616 | bytes 2162688 | tf_op jit(solution)/shard_map/while/body/eval_jaxpr/tqi,bif->btqf/dot_general | solution.py:55
  42.6 3.9 %scatter_fusion = f32[416,512]{1,0:T(8,128)S(1)} fusion(f32[416,512]{1,0:T(8,128)S(1)} %get-tuple-element.213, s32[512]{0:T(512)S(1)} %bitcast.110, f32[512,512]{1,0:T(8,128)S(1)} %copy.51), kind=kCustom, calls=%fused_computation.1.clone.1 | custom fusion | flops 262144 | bytes 3147776 | tf_op jit(solution)/shard_map/while/body/eval_jaxpr/scatter-add | solution.py:63
  47.3 2.9 %collective-permute-start.5 = (bf16[1,16,512]{2,1,0:T(8,128)(2,1)}, bf16[1,16,512]{2,1,0:T(8,128)(2,1)}, u32[]{:S(2)}, u32[]{:S(2)}) collective-permute-start(bf16[1,16,512]{2,1,0:T(8,128)(2,1)} %get-tuple-element.114), channel_id=1, source_target_pairs={{16,0},{0,16},{17,1},{1,17},{18,2},{2,18},{19,3},{3,19},{20,4},{4,... | collective-permute-start | bytes 49160 | tf_op jit(solution)/shard_map/ppermute | solution.py:16
  50.9 4.4 %collective-permute-start.1 = (bf16[1,3,16,512]{3,2,1,0:T(8,128)(2,1)}, bf16[1,3,16,512]{3,2,1,0:T(8,128)(2,1)}, u32[]{:S(2)}, u32[]{:S(2)}) collective-permute-start(bf16[1,3,16,512]{3,2,1,0:T(8,128)(2,1)} %maximum_bitcast_fusion.1), channel_id=1, source_target_pairs={{1,0},{2,1},{3,2},{4,3},{5,4},{6,5},{7,6},{8,7},{9,8},{10,9},{11,1... | collective-permute-start | bytes 147464 | tf_op jit(solution)/shard_map/ppermute | solution.py:16
  55.4 3.3 %copy.31 = bf16[256,4096]{0,1:T(8,128)(2,1)S(1)} copy(bf16[256,4096]{1,0:T(8,128)(2,1)} %param.21) | data formatting | bytes 4194304 | tf_op args[9]
  58.7 6.7 %copy.33 = bf16[256,64,64]{2,1,0:T(8,128)(2,1)} copy(bf16[256,64,64]{0,2,1:T(8,128)(2,1)S(1)} %bitcast.107) | data formatting | bytes 4194304 | tf_op jit(solution)/shard_map/reshape | solution.py:112
  67.2 3.6 %collective-permute-start.3 = (bf16[3,16,512]{2,1,0:T(8,128)(2,1)S(1)}, bf16[3,16,512]{2,1,0:T(8,128)(2,1)S(1)}, u32[]{:S(2)}, u32[]{:S(2)}) collective-permute-start(bf16[3,16,512]{2,1,0:T(8,128)(2,1)S(1)} %pad_maximum_fusion.1), channel_id=1, source_target_pairs={{4,0},{5,1},{6,2},{7,3},{8,4},{9,5},{10,6},{11,7},{12,8},{13,9},{1... | collective-permute-start | bytes 147464 | tf_op jit(solution)/shard_map/ppermute | solution.py:24
  74.4 1.9 %scatter_custom_fusion.1 = f32[256,512]{1,0:T(8,128)S(1)} fusion(f32[256,512]{1,0:T(8,128)S(1)} %slice.129, s32[160]{0:T(256)} %bitcast.116, bf16[160,512]{1,0:T(8,128)(2,1)S(1)} %bitcast.115), kind=kCustom, calls=%fused_computation.29 | custom fusion | flops 163840 | bytes 688128 | tf_op jit(solution)/shard_map/scatter-add | solution.py:108
  76.9 4.4 %convolution_bitcast_fusion = f32[256,64,8]{1,2,0:T(8,128)S(1)} fusion(bf16[256,64,8]{1,2,0:T(8,128)(2,1)S(1)} %copy.32, bf16[256,64,64]{2,1,0:T(8,128)(2,1)} %copy.33), kind=kOutput, calls=%fused_computation.28 | convolution fusion | flops 16777216 | bytes 2883584 | tf_op jit(solution)/shard_map/zjk,zkf->zjf/dot_general | solution.py:113
  81.8 1.0 %copy.35 = f32[256,512]{1,0:T(8,128)} copy(f32[256,512]{0,1:T(8,128)S(1)} %bitcast.108) | data formatting | bytes 1048576 | tf_op jit(solution)/shard_map/reshape | solution.py:114
  (99 shorter events, 18.3 us)
Async XLA Ops:
  4.0 3.4 %copy-start = (f32[8,64]{1,0:T(8,128)S(1)}, f32[8,64]{1,0:T(8,128)}, u32[]{:S(2)}) copy-start(f32[8,64]{1,0:T(8,128)} %get-tuple-element.227) | copy-start | bytes 6148 | tf_op jit(solution)/shard_map/while
  4.0 3.5 %copy-start.1 = (bf16[8,64,64]{2,1,0:T(8,128)(2,1)S(1)}, bf16[8,64,64]{2,1,0:T(8,128)(2,1)}, u32[]{:S(2)}) copy-start(bf16[8,64,64]{2,1,0:T(8,128)(2,1)} %get-tuple-element.231) | copy-start | bytes 196612 | tf_op jit(solution)/shard_map/while
  14.6 3.4 %copy-start = (f32[8,64]{1,0:T(8,128)S(1)}, f32[8,64]{1,0:T(8,128)}, u32[]{:S(2)}) copy-start(f32[8,64]{1,0:T(8,128)} %get-tuple-element.227) | copy-start | bytes 6148 | tf_op jit(solution)/shard_map/while
  14.6 3.5 %copy-start.1 = (bf16[8,64,64]{2,1,0:T(8,128)(2,1)S(1)}, bf16[8,64,64]{2,1,0:T(8,128)(2,1)}, u32[]{:S(2)}) copy-start(bf16[8,64,64]{2,1,0:T(8,128)(2,1)} %get-tuple-element.231) | copy-start | bytes 196612 | tf_op jit(solution)/shard_map/while
  25.3 3.4 %copy-start = (f32[8,64]{1,0:T(8,128)S(1)}, f32[8,64]{1,0:T(8,128)}, u32[]{:S(2)}) copy-start(f32[8,64]{1,0:T(8,128)} %get-tuple-element.227) | copy-start | bytes 6148 | tf_op jit(solution)/shard_map/while
  25.3 3.5 %copy-start.1 = (bf16[8,64,64]{2,1,0:T(8,128)(2,1)S(1)}, bf16[8,64,64]{2,1,0:T(8,128)(2,1)}, u32[]{:S(2)}) copy-start(bf16[8,64,64]{2,1,0:T(8,128)(2,1)} %get-tuple-element.231) | copy-start | bytes 196612 | tf_op jit(solution)/shard_map/while
  35.9 3.4 %copy-start = (f32[8,64]{1,0:T(8,128)S(1)}, f32[8,64]{1,0:T(8,128)}, u32[]{:S(2)}) copy-start(f32[8,64]{1,0:T(8,128)} %get-tuple-element.227) | copy-start | bytes 6148 | tf_op jit(solution)/shard_map/while
  35.9 3.5 %copy-start.1 = (bf16[8,64,64]{2,1,0:T(8,128)(2,1)S(1)}, bf16[8,64,64]{2,1,0:T(8,128)(2,1)}, u32[]{:S(2)}) copy-start(bf16[8,64,64]{2,1,0:T(8,128)(2,1)} %get-tuple-element.231) | copy-start | bytes 196612 | tf_op jit(solution)/shard_map/while
  47.3 26.4 %collective-permute-start.5 = (bf16[1,16,512]{2,1,0:T(8,128)(2,1)}, bf16[1,16,512]{2,1,0:T(8,128)(2,1)}, u32[]{:S(2)}, u32[]{:S(2)}) collective-permute-start(bf16[1,16,512]{2,1,0:T(8,128)(2,1)} %get-tuple-element.114), channel_id=1, source_target_pairs={{16,0},{0,16},{17,1},{1,17},{18,2},{2,18},{19,3},{3,19},{20,4},{4,... | collective-permute-start | bytes 49160 | tf_op jit(solution)/shard_map/ppermute | solution.py:16
  50.2 22.8 %collective-permute-start.4 = (bf16[1,16,512]{2,1,0:T(8,128)(2,1)}, bf16[1,16,512]{2,1,0:T(8,128)(2,1)}, u32[]{:S(2)}, u32[]{:S(2)}) collective-permute-start(bf16[1,16,512]{2,1,0:T(8,128)(2,1)} %get-tuple-element.115), channel_id=1, source_target_pairs={{0,16},{16,0},{1,17},{17,1},{2,18},{18,2},{3,19},{19,3},{4,20},{20... | collective-permute-start | bytes 49160 | tf_op jit(solution)/shard_map/ppermute | solution.py:13
  50.2 15.1 %collective-permute-start = (bf16[1,3,16,512]{3,2,1,0:T(8,128)(2,1)S(1)}, bf16[1,3,16,512]{3,2,1,0:T(8,128)(2,1)}, u32[]{:S(2)}, u32[]{:S(2)}) collective-permute-start(bf16[1,3,16,512]{3,2,1,0:T(8,128)(2,1)S(1)} %maximum_bitcast_fusion), channel_id=1, source_target_pairs={{0,1},{1,2},{2,3},{3,4},{4,5},{5,6},{6,7},{7,8},{8,9},{9,10},{10,1... | collective-permute-start | bytes 147464 | tf_op jit(solution)/shard_map/ppermute | solution.py:13
  50.9 15.2 %collective-permute-start.1 = (bf16[1,3,16,512]{3,2,1,0:T(8,128)(2,1)}, bf16[1,3,16,512]{3,2,1,0:T(8,128)(2,1)}, u32[]{:S(2)}, u32[]{:S(2)}) collective-permute-start(bf16[1,3,16,512]{3,2,1,0:T(8,128)(2,1)} %maximum_bitcast_fusion.1), channel_id=1, source_target_pairs={{1,0},{2,1},{3,2},{4,3},{5,4},{6,5},{7,6},{8,7},{9,8},{10,9},{11,1... | collective-permute-start | bytes 147464 | tf_op jit(solution)/shard_map/ppermute | solution.py:16
  66.9 6.0 %collective-permute-start.2 = (bf16[3,16,512]{2,1,0:T(8,128)(2,1)S(1)}, bf16[3,16,512]{2,1,0:T(8,128)(2,1)S(1)}, u32[]{:S(2)}, u32[]{:S(2)}) collective-permute-start(bf16[3,16,512]{2,1,0:T(8,128)(2,1)S(1)} %pad_maximum_fusion), channel_id=1, source_target_pairs={{12,0},{13,1},{14,2},{15,3},{0,4},{1,5},{2,6},{3,7},{4,8},{5,9},{6... | collective-permute-start | bytes 147464 | tf_op jit(solution)/shard_map/ppermute | solution.py:24
  67.2 5.7 %collective-permute-start.3 = (bf16[3,16,512]{2,1,0:T(8,128)(2,1)S(1)}, bf16[3,16,512]{2,1,0:T(8,128)(2,1)S(1)}, u32[]{:S(2)}, u32[]{:S(2)}) collective-permute-start(bf16[3,16,512]{2,1,0:T(8,128)(2,1)S(1)} %pad_maximum_fusion.1), channel_id=1, source_target_pairs={{4,0},{5,1},{6,2},{7,3},{8,4},{9,5},{10,6},{11,7},{12,8},{13,9},{1... | collective-permute-start | bytes 147464 | tf_op jit(solution)/shard_map/ppermute | solution.py:24
where the time goes:
time: 84 us; the launch traced here: 82.8 us
  local copies, waits for them, and re-layouts  37.6 us (45%)
  other arithmetic  19.3 us (23%)
  matrix products  13.2 us (16%)
  starting transfers between devices  11.4 us (14%)
    scatter-add x4, other arithmetic, quad_block(): jax.ops.segment_sum(moment.reshape(block_rows, row_width), dest_blk, num_...  15.7 us
    gather x8, local copies, waits for them, and re-layouts, quad_block(): jnp.take(old_coeff, zone_blk, axis=0)  12.7 us
    ppermute x2, starting transfers between devices, extended_2(): lax.ppermute(lax.slice_in_dim(block, 0, width, axis=dim), axis, backward)  7.36 us
    reshape x1, local copies, waits for them, and re-layouts, on_device(): inverse = inv_mass.reshape(zone_count, basis_size, basis_size)  6.69 us
    unnamed x10, local copies, waits for them, and re-layouts  5.45 us
    dot_general x4, matrix products, quad_block(): jnp.einsum('tqi,bif->btqf', basis_old, picked, preferred_element_type=jnp...  5.11 us
    dot_general x1, matrix products, on_device(): jnp.einsum('zjk,zkf->zjf', inverse, rounded, preferred_element_type=jnp.f...  4.43 us
    ppermute x2, starting transfers between devices, passed_along(): return lax.ppermute(block, axis, route)  3.93 us
  transfers between devices with their start and end apart: 6, of which 1 were waited for; matrix products, arithmetic and copies ran while one was open for 17% of the time, Pallas kernels for 0%

commit v1 on v0

v1 whole, which is shorter than its diff:
```python
import functools

import jax
import jax.numpy as jnp
from jax import lax
from jax.experimental import pallas as pl
from jax.experimental.pallas import tpu as pltpu
from jax.sharding import PartitionSpec as P

BF = jnp.bfloat16
F32 = jnp.float32
PARTNERS = 10


def nn(left, right):
    return lax.dot_general(left, right, (((1,), (0,)), ((), ())), preferred_element_type=F32)


def nt(left, right):
    return lax.dot_general(left, right, (((1,), (1,)), ((), ())), preferred_element_type=F32)


def halves(value):
    high = value.astype(BF)
    return high, (value - high.astype(F32)).astype(BF)


def iotas(shape):
    return lax.broadcasted_iota(jnp.int32, shape, 0), lax.broadcasted_iota(jnp.int32, shape, 1)


def one_hot(mask):
    return jnp.where(mask, 1.0, 0.0).astype(BF)


def kernel(
    old_ref,
    bold_ref,
    bnew_ref,
    weight_ref,
    zone_ref,
    table_ref,
    volume_ref,
    dest_ref,
    list_ref,
    mass_hbm,
    out_ref,
    mass_ref,
    sent_ref,
    recv_ref,
    perm_ref,
    moved_ref,
    picked_ref,
    dest_hot_ref,
    mass_t_ref,
    gath_t_ref,
    out_t_ref,
    mass_sem,
    send_sem,
    recv_sem,
):
    zones, width = old_ref.shape
    tables, quads, nb = bold_ref.shape
    nf = width // nb
    tets = zone_ref.shape[1]
    slots = list_ref.shape[1]
    cap = slots // PARTNERS
    rows = zones + slots

    mass_copy = pltpu.make_async_copy(mass_hbm, mass_ref, mass_sem)
    mass_copy.start()

    a, b = lax.axis_index("gx"), lax.axis_index("yz")
    n_a, n_b = lax.axis_size("gx"), lax.axis_size("yz")
    face = 1 << (n_b.bit_length() - 1) // 2
    offsets = (1, -1, face, -face, face + 1, -face - 1, face - 1, 1 - face)
    partners = [(a, lax.rem(b + (o + n_b), n_b)) for o in offsets]
    partners += [(lax.rem(a + 1, n_a), b), (lax.rem(a + n_a - 1, n_a), b)]
    barrier = pltpu.get_barrier_semaphore()
    for where in partners:
        pl.semaphore_signal(
            barrier, inc=1, device_id=where, device_id_type=pl.DeviceIdType.MESH
        )

    r, c = iotas((width, width))
    perm_ref[...] = one_hot(r == (c % nb) * nf + c // nb)
    perm = perm_ref[...]

    coeff = nn(old_ref[...], perm).astype(BF)
    quad = 4 * nb
    r, c = iotas((nb, quad))
    bnew4 = nn(bnew_ref[...].reshape(tables * quads, nb), one_hot(r == c % nb)).astype(BF)
    r, c = iotas((nb, nb))
    eye_nb = one_hot(r == c)
    r, c = iotas((quad, quad))
    same = r // nb == c // nb
    for t in range(tables):
        high, low = halves(nt(eye_nb, bold_ref[t]) * weight_ref[t : t + 1, :])
        new_t = bnew4[t * quads : (t + 1) * quads]
        both = nn(high, new_t) + nn(low, new_t)
        block = jnp.where(same, jnp.concatenate([both] * 4, axis=0), 0.0)
        high, low = halves(block)
        for h in range(width // quad):
            part = coeff[:, h * quad : (h + 1) * quad]
            moved_ref[t * zones : (t + 1) * zones, h * quad : (h + 1) * quad] = (
                nn(part, high) + nn(part, low)
            ).astype(BF)

    r, _ = iotas((rows, tets))
    dest_hot_ref[...] = jnp.where(dest_ref[...] == r, volume_ref[...], 0.0).astype(BF)
    r, _ = iotas((zones, tets))
    for t in range(tables):
        of_table = jnp.where(table_ref[...] == t, zone_ref[...], -1)
        picked_ref[:, t * zones : (t + 1) * zones] = nt(
            dest_hot_ref[...], one_hot(of_table == r)
        ).astype(BF)

    sent_ref[...] = nn(picked_ref[zones:, :], moved_ref[...]).astype(BF)
    pl.semaphore_wait(barrier, PARTNERS)
    copies = []
    for k, where in enumerate(partners):
        copy = pltpu.make_async_remote_copy(
            src_ref=sent_ref.at[k * cap : (k + 1) * cap],
            dst_ref=recv_ref.at[k * cap : (k + 1) * cap],
            send_sem=send_sem.at[k],
            recv_sem=recv_sem.at[k],
            device_id=where,
            device_id_type=pl.DeviceIdType.MESH,
        )
        copy.start()
        copies.append(copy)

    own = nn(picked_ref[:zones, :], moved_ref[...])
    mass_copy.wait()
    for o in range(nb // nf):
        mass_t_ref[o * width : (o + 1) * width, :] = nt(
            perm, mass_ref[:, o * width : (o + 1) * width]
        )
    r, _ = iotas((zones, slots))
    list_hot = one_hot(list_ref[...] == r)

    for copy in copies:
        copy.wait()
    gathered = own + nn(list_hot, recv_ref[...])
    gath_t_ref[...] = nt(perm, gathered.astype(BF))

    lanes = 128
    group = 4
    octets = nb // nf
    per_step = 4
    for h in range(zones // lanes):
        at = slice(h * lanes, (h + 1) * lanes)
        for f0 in range(0, nf, group):

            def step(i, sums):
                sums = list(sums)
                for u in range(per_step):
                    base = pl.multiple_of((i * per_step + u) * nf, nf)
                    column = gath_t_ref[pl.ds(base, nf), at]
                    for o in range(octets):
                        mass = mass_t_ref[pl.ds(o * width + base, nf), at]
                        for f in range(group):
                            sums[o * group + f] += mass * column[f0 + f : f0 + f + 1, :]
                return tuple(sums)

            start = tuple(jnp.zeros((nf, lanes), F32) for _ in range(octets * group))
            sums = lax.fori_loop(0, nb // per_step, step, start)
            for o in range(octets):
                for f in range(group):
                    out_t_ref[h, pl.ds(o * nf * nf + f0 + f, nf, stride=nf), :] = sums[
                        o * group + f
                    ]

    r, c = iotas((lanes, lanes))
    eye = one_hot(r == c)
    for h in range(zones // lanes):
        high, low = halves(out_t_ref[h])
        out_ref[h * lanes : (h + 1) * lanes, :] = nt(eye, high) + nt(eye, low)


def on_device(
    old_coeff,
    basis_old,
    basis_new,
    quad_weight,
    tet_zone,
    tet_table,
    tet_volume,
    tet_dest,
    recv_list,
    inv_mass,
):
    zones, width = old_coeff.shape
    tables = basis_old.shape[0]
    nb = basis_old.shape[2]
    tets = tet_zone.shape[0]
    slots = recv_list.shape[1]
    rows = zones + slots
    in_vmem = pl.BlockSpec(memory_space=pltpu.VMEM)
    return pl.pallas_call(
        kernel,
        out_shape=jax.ShapeDtypeStruct((zones, width), F32),
        in_specs=[in_vmem] * 9 + [pl.BlockSpec(memory_space=pl.ANY)],
        out_specs=in_vmem,
        scratch_shapes=[
            pltpu.VMEM(inv_mass.shape, BF),
            pltpu.VMEM((slots, width), BF),
            pltpu.VMEM((slots, width), BF),
            pltpu.VMEM((width, width), BF),
            pltpu.VMEM((tables * zones, width), BF),
            pltpu.VMEM((rows, tables * zones), BF),
            pltpu.VMEM((rows, tets), BF),
            pltpu.VMEM((nb * nb, zones), F32),
            pltpu.VMEM((width, zones), F32),
            pltpu.VMEM((zones // 128, width, 128), F32),
            pltpu.SemaphoreType.DMA,
            pltpu.SemaphoreType.DMA((PARTNERS,)),
            pltpu.SemaphoreType.DMA((PARTNERS,)),
        ],
        compiler_params=pltpu.CompilerParams(
            collective_id=0, has_side_effects=True, vmem_limit_bytes=52 * 2**20
        ),
    )(
        old_coeff,
        basis_old,
        basis_new,
        quad_weight,
        tet_zone.reshape(1, tets),
        tet_table.reshape(1, tets),
        tet_volume.reshape(1, tets),
        tet_dest.reshape(1, tets),
        recv_list,
        inv_mass,
    )


def solution(mesh):
    placed = (
        P(("gx", "yz"), None),
        P(),
        P(),
        P(),
        P(("gx", "yz")),
        P(("gx", "yz")),
        P(("gx", "yz")),
        P(("gx", "yz")),
        P(("gx", "yz"), None),
        P(("gx", "yz"), None),
    )
    return jax.shard_map(
        on_device, mesh=mesh, in_specs=placed, out_specs=P(("gx", "yz"), None), check_vma=False
    )
```

time: 84 us -> 28.8 us (0.34)
  the two profiles are of different devices: /device:TPU:0 before, /device:TPU:1 now
where the time goes in v1:
time: 28.8 us; the launch traced here: 28.4 us
  Pallas kernels  20.6 us (72%)
  local copies, waits for them, and re-layouts  7.7 us (27%)
    pallas_call x1, Pallas kernels, on_device(): pl.pallas_call(kernel, out_shape=jax.ShapeDtypeStruct((zones, width), F32...  20.6 us
    unnamed x19, local copies, waits for them, and re-layouts  7.7 us

profile of v1, /device:TPU:1, one launch (start us, length us, event | category | flops | bytes accessed | tf_op | source)
XLA Modules:
  0.0 28.4 jit_solution(3436129465255299364)
XLA Ops:
  0.0 0.0 copy-start
  0.0 0.9 %copy-done = bf16[256,512]{1,0:T(8,128)(2,1)S(1)} copy-done((bf16[256,512]{1,0:T(8,128)(2,1)S(1)}, bf16[256,512]{1,0:T(8,128)(2,1)}, u32[]{:S(2)}) %copy-start) | copy-done | bytes 262168
  1.0 0.0 copy-start.1
  1.0 0.9 %copy-done.1 = bf16[8,64,64]{2,1,0:T(8,128)(2,1)S(1)} copy-done((bf16[8,64,64]{2,1,0:T(8,128)(2,1)S(1)}, bf16[8,64,64]{2,1,0:T(8,128)(2,1)}, u32[]{:S(2)}) %copy-start.1) | copy-done | bytes 65560
  1.9 0.0 copy-start.2
  1.9 0.9 %copy-done.2 = bf16[8,64,64]{2,1,0:T(8,128)(2,1)S(1)} copy-done((bf16[8,64,64]{2,1,0:T(8,128)(2,1)S(1)}, bf16[8,64,64]{2,1,0:T(8,128)(2,1)}, u32[]{:S(2)}) %copy-start.2) | copy-done | bytes 65560
  2.8 0.0 copy-start.3
  2.8 0.7 %copy-done.3 = s32[2048]{0:T(1024)S(1)} copy-done((s32[2048]{0:T(1024)S(1)}, s32[2048]{0:T(1024)}, u32[]{:S(2)}) %copy-start.3) | copy-done | bytes 8216
  3.5 0.0 copy-start.4
  3.5 0.7 %copy-done.4 = s32[2048]{0:T(1024)S(1)} copy-done((s32[2048]{0:T(1024)S(1)}, s32[2048]{0:T(1024)}, u32[]{:S(2)}) %copy-start.4) | copy-done | bytes 8216
  4.2 0.0 copy-start.5
  4.2 0.7 %copy-done.5 = f32[2048]{0:T(1024)S(1)} copy-done((f32[2048]{0:T(1024)S(1)}, f32[2048]{0:T(1024)}, u32[]{:S(2)}) %copy-start.5) | copy-done | bytes 8216
  4.9 0.0 copy-start.6
  4.9 0.7 %copy-done.6 = s32[2048]{0:T(1024)S(1)} copy-done((s32[2048]{0:T(1024)S(1)}, s32[2048]{0:T(1024)}, u32[]{:S(2)}) %copy-start.6) | copy-done | bytes 8216
  5.5 0.0 copy-start.7
  5.6 0.7 %copy-done.7 = f32[8,64]{1,0:T(8,128)S(1)} copy-done((f32[8,64]{1,0:T(8,128)S(1)}, f32[8,64]{1,0:T(8,128)}, u32[]{:S(2)}) %copy-start.7) | copy-done | bytes 2072
  6.2 0.0 copy-start.8
  6.2 0.7 %copy-done.8 = s32[1,160]{1,0:T(1,128)S(1)} copy-done((s32[1,160]{1,0:T(1,128)S(1)}, s32[1,160]{1,0:T(1,128)}, u32[]{:S(2)}) %copy-start.8) | copy-done | bytes 664
  6.9 20.6 %shard_map.100 = f32[256,512]{1,0:T(8,128)S(1)} custom-call(bf16[256,512]{1,0:T(8,128)(2,1)S(1)} %copy-done, bf16[8,64,64]{2,1,0:T(8,128)(2,1)S(1)} %copy-done.1, bf16[8,64,64]{2,1,0:T(8,128)(2,1)S(1)} %copy-done.2, f32[8,64]{1,0:T(8,128)S(1)} %copy-done.7, s32[1,2048]{1,0:T(1,128)S(1)} %bitcast.4, s32[1,2048]{1,0:T(1,128)S(1)} %bitcast.5, ...), custom_call_target="tpu_custom_call" | custom-call | tf_op jit(solution)/shard_map/pallas_call | solution.py:200
  27.6 0.8 %copy.12 = f32[256,512]{1,0:T(8,128)} copy(f32[256,512]{1,0:T(8,128)S(1)} %shard_map.100) | data formatting | bytes 1048576
Async XLA Ops:
  0.0 0.9 %copy-start = (bf16[256,512]{1,0:T(8,128)(2,1)S(1)}, bf16[256,512]{1,0:T(8,128)(2,1)}, u32[]{:S(2)}) copy-start(bf16[256,512]{1,0:T(8,128)(2,1)} %old_ref.1) | copy-start | bytes 786436
  1.0 0.9 %copy-start.1 = (bf16[8,64,64]{2,1,0:T(8,128)(2,1)S(1)}, bf16[8,64,64]{2,1,0:T(8,128)(2,1)}, u32[]{:S(2)}) copy-start(bf16[8,64,64]{2,1,0:T(8,128)(2,1)} %bold_ref.1) | copy-start | bytes 196612
  1.9 0.9 %copy-start.2 = (bf16[8,64,64]{2,1,0:T(8,128)(2,1)S(1)}, bf16[8,64,64]{2,1,0:T(8,128)(2,1)}, u32[]{:S(2)}) copy-start(bf16[8,64,64]{2,1,0:T(8,128)(2,1)} %bnew_ref.1) | copy-start | bytes 196612
  2.8 0.7 %copy-start.3 = (s32[2048]{0:T(1024)S(1)}, s32[2048]{0:T(1024)}, u32[]{:S(2)}) copy-start(s32[2048]{0:T(1024)} %param.14) | copy-start | bytes 24580
  3.5 0.7 %copy-start.4 = (s32[2048]{0:T(1024)S(1)}, s32[2048]{0:T(1024)}, u32[]{:S(2)}) copy-start(s32[2048]{0:T(1024)} %param.15) | copy-start | bytes 24580
  4.2 0.7 %copy-start.5 = (f32[2048]{0:T(1024)S(1)}, f32[2048]{0:T(1024)}, u32[]{:S(2)}) copy-start(f32[2048]{0:T(1024)} %param.16) | copy-start | bytes 24580
  4.9 0.7 %copy-start.6 = (s32[2048]{0:T(1024)S(1)}, s32[2048]{0:T(1024)}, u32[]{:S(2)}) copy-start(s32[2048]{0:T(1024)} %param.17) | copy-start | bytes 24580
  5.5 0.7 %copy-start.7 = (f32[8,64]{1,0:T(8,128)S(1)}, f32[8,64]{1,0:T(8,128)}, u32[]{:S(2)}) copy-start(f32[8,64]{1,0:T(8,128)} %weight_ref.1) | copy-start | bytes 6148
  6.2 0.7 %copy-start.8 = (s32[1,160]{1,0:T(1,128)S(1)}, s32[1,160]{1,0:T(1,128)}, u32[]{:S(2)}) copy-start(s32[1,160]{1,0:T(1,128)} %list_ref.1) | copy-start | bytes 1924

commit v2 on v1

--- a/solution.py
+++ b/solution.py
@@ -34,6 +34,17 @@
 
 
 def kernel(
+    old_hbm,
+    bold_hbm,
+    bnew_hbm,
+    weight_hbm,
+    zone_hbm,
+    table_hbm,
+    volume_hbm,
+    dest_hbm,
+    list_hbm,
+    mass_hbm,
+    out_ref,
     old_ref,
     bold_ref,
     bnew_ref,
@@ -43,8 +54,6 @@
     volume_ref,
     dest_ref,
     list_ref,
-    mass_hbm,
-    out_ref,
     mass_ref,
     sent_ref,
     recv_ref,
@@ -55,7 +64,7 @@
     mass_t_ref,
     gath_t_ref,
     out_t_ref,
-    mass_sem,
+    in_sem,
     send_sem,
     recv_sem,
 ):
@@ -67,8 +76,24 @@
     cap = slots // PARTNERS
     rows = zones + slots
 
-    mass_copy = pltpu.make_async_copy(mass_hbm, mass_ref, mass_sem)
-    mass_copy.start()
+    pairs = (
+        (bnew_hbm, bnew_ref),
+        (bold_hbm, bold_ref),
+        (weight_hbm, weight_ref),
+        (dest_hbm, dest_ref),
+        (volume_hbm, volume_ref),
+        (zone_hbm, zone_ref),
+        (table_hbm, table_ref),
+        (old_hbm, old_ref),
+        (list_hbm, list_ref),
+        (mass_hbm, mass_ref),
+    )
+    loads = [
+        pltpu.make_async_copy(source, target, in_sem.at[i])
+        for i, (source, target) in enumerate(pairs)
+    ]
+    for load in loads:
+        load.start()
 
     a, b = lax.axis_index("gx"), lax.axis_index("yz")
     n_a, n_b = lax.axis_size("gx"), lax.axis_size("yz")
@@ -86,6 +111,8 @@
     perm_ref[...] = one_hot(r == (c % nb) * nf + c // nb)
     perm = perm_ref[...]
 
+    for load in loads[:8]:
+        load.wait()
     coeff = nn(old_ref[...], perm).astype(BF)
     quad = 4 * nb
     r, c = iotas((nb, quad))
@@ -99,20 +126,25 @@
         new_t = bnew4[t * quads : (t + 1) * quads]
         both = nn(high, new_t) + nn(low, new_t)
         block = jnp.where(same, jnp.concatenate([both] * 4, axis=0), 0.0)
-        high, low = halves(block)
+        block = block.astype(BF)
         for h in range(width // quad):
             part = coeff[:, h * quad : (h + 1) * quad]
-            moved_ref[t * zones : (t + 1) * zones, h * quad : (h + 1) * quad] = (
-                nn(part, high) + nn(part, low)
+            moved_ref[t * zones : (t + 1) * zones, h * quad : (h + 1) * quad] = nn(
+                part, block
             ).astype(BF)
 
-    r, _ = iotas((rows, tets))
-    dest_hot_ref[...] = jnp.where(dest_ref[...] == r, volume_ref[...], 0.0).astype(BF)
-    r, _ = iotas((zones, tets))
+    numbers = iotas((zones, tets))[0].astype(F32).astype(BF)
+    one, zero = jnp.ones((), BF), jnp.zeros((), BF)
+    volume = volume_ref[...].astype(BF)
+    dest = dest_ref[...]
+    own_zone = jnp.where(dest < zones, dest, -1).astype(F32).astype(BF)
+    far_slot = jnp.where(dest < zones, -1, dest - zones).astype(F32).astype(BF)
+    dest_hot_ref[:zones, :] = jnp.where(own_zone == numbers, volume, zero)
+    dest_hot_ref[zones:, :] = jnp.where(far_slot == numbers[:slots], volume, zero)
     for t in range(tables):
-        of_table = jnp.where(table_ref[...] == t, zone_ref[...], -1)
+        of_table = jnp.where(table_ref[...] == t, zone_ref[...], -1).astype(F32).astype(BF)
         picked_ref[:, t * zones : (t + 1) * zones] = nt(
-            dest_hot_ref[...], one_hot(of_table == r)
+            dest_hot_ref[...], jnp.where(of_table == numbers, one, zero)
         ).astype(BF)
 
     sent_ref[...] = nn(picked_ref[zones:, :], moved_ref[...]).astype(BF)
@@ -131,18 +163,20 @@
         copies.append(copy)
 
     own = nn(picked_ref[:zones, :], moved_ref[...])
-    mass_copy.wait()
+    loads[9].wait()
     for o in range(nb // nf):
         mass_t_ref[o * width : (o + 1) * width, :] = nt(
             perm, mass_ref[:, o * width : (o + 1) * width]
         )
+    loads[8].wait()
     r, _ = iotas((zones, slots))
     list_hot = one_hot(list_ref[...] == r)
 
     for copy in copies:
         copy.wait()
     gathered = own + nn(list_hot, recv_ref[...])
-    gath_t_ref[...] = nt(perm, gathered.astype(BF))
+    high, low = halves(gathered)
+    gath_t_ref[...] = nt(perm, high) + nt(perm, low)
 
     lanes = 128
     group = 4
@@ -196,31 +230,7 @@
     tets = tet_zone.shape[0]
     slots = recv_list.shape[1]
     rows = zones + slots
-    in_vmem = pl.BlockSpec(memory_space=pltpu.VMEM)
-    return pl.pallas_call(
-        kernel,
-        out_shape=jax.ShapeDtypeStruct((zones, width), F32),
-        in_specs=[in_vmem] * 9 + [pl.BlockSpec(memory_space=pl.ANY)],
-        out_specs=in_vmem,
-        scratch_shapes=[
-            pltpu.VMEM(inv_mass.shape, BF),
-            pltpu.VMEM((slots, width), BF),
-            pltpu.VMEM((slots, width), BF),
-            pltpu.VMEM((width, width), BF),
-            pltpu.VMEM((tables * zones, width), BF),
-            pltpu.VMEM((rows, tables * zones), BF),
-            pltpu.VMEM((rows, tets), BF),
-            pltpu.VMEM((nb * nb, zones), F32),
-            pltpu.VMEM((width, zones), F32),
-            pltpu.VMEM((zones // 128, width, 128), F32),
-            pltpu.SemaphoreType.DMA,
-            pltpu.SemaphoreType.DMA((PARTNERS,)),
-            pltpu.SemaphoreType.DMA((PARTNERS,)),
-        ],
-        compiler_params=pltpu.CompilerParams(
-            collective_id=0, has_side_effects=True, vmem_limit_bytes=52 * 2**20
-        ),
-    )(
+    operands = (
         old_coeff,
         basis_old,
         basis_new,
@@ -232,6 +242,30 @@
         recv_list,
         inv_mass,
     )
+    return pl.pallas_call(
+        kernel,
+        out_shape=jax.ShapeDtypeStruct((zones, width), F32),
+        in_specs=[pl.BlockSpec(memory_space=pltpu.HBM)] * len(operands),
+        out_specs=pl.BlockSpec(memory_space=pltpu.VMEM),
+        scratch_shapes=[
+            *(pltpu.VMEM(x.shape, x.dtype) for x in operands),
+            pltpu.VMEM((slots, width), BF),
+            pltpu.VMEM((slots, width), BF),
+            pltpu.VMEM((width, width), BF),
+            pltpu.VMEM((tables * zones, width), BF),
+            pltpu.VMEM((rows, tables * zones), BF),
+            pltpu.VMEM((rows, tets), BF),
+            pltpu.VMEM((nb * nb, zones), F32),
+            pltpu.VMEM((width, zones), F32),
+            pltpu.VMEM((zones // 128, width, 128), F32),
+            pltpu.SemaphoreType.DMA((len(operands),)),
+            pltpu.SemaphoreType.DMA((PARTNERS,)),
+            pltpu.SemaphoreType.DMA((PARTNERS,)),
+        ],
+        compiler_params=pltpu.CompilerParams(
+            collective_id=0, has_side_effects=True, vmem_limit_bytes=62 * 2**20
+        ),
+    )(*operands)
 
 
 def solution(mesh):

time: 28.8 us -> 24 us (0.83); the launches traced: 28.4 us -> 23.9 us
  local copies, waits for them, and re-layouts: 7.7 us -> 1.87 us
  Pallas kernels: 20.6 us -> 22 us
    unnamed x19 -> x1, local copies, waits for them, and re-layouts: 7.7 us -> 1.87 us
    pallas_call x1, Pallas kernels: 20.6 us -> 22 us  [on_device(): pl.pallas_call(kernel, out_shape=jax.ShapeDtypeStruct((zones, width), F32...]
where the time goes in v2:
time: 24 us; the launch traced here: 23.9 us
  Pallas kernels  22 us (92%)
  local copies, waits for them, and re-layouts  1.87 us (8%)
    pallas_call x1, Pallas kernels, on_device(): pl.pallas_call(kernel, out_shape=jax.ShapeDtypeStruct((zones, width), F32...  22 us
    unnamed x1, local copies, waits for them, and re-layouts  1.87 us

profile of v2, /device:TPU:1, one launch (start us, length us, event | category | flops | bytes accessed | tf_op | source)
XLA Modules:
  0.0 23.9 jit_solution(6718114526857445245)
XLA Ops:
  0.0 22.0 %shard_map.100 = f32[256,512]{1,0:T(8,128)} custom-call(bf16[256,512]{1,0:T(8,128)(2,1)} %old_hbm.1, bf16[8,64,64]{2,1,0:T(8,128)(2,1)} %bold_hbm.1, bf16[8,64,64]{2,1,0:T(8,128)(2,1)} %bnew_hbm.1, f32[8,64]{1,0:T(8,128)} %weight_hbm.1, s32[1,2048]{1,0:T(1,128)} %bitcast.4, s32[1,2048]{1,0:T(1,128)} %bitcast.5, f32[1,2048]{1,0:T(1,128)} %bitcast.6, ...), custom_call_target="tpu_custom_call" | custom-call | tf_op jit(solution)/shard_map/pallas_call | solution.py:245
  22.0 1.9 %copy.12 = f32[256,512]{1,0:T(8,128)} copy(f32[256,512]{1,0:T(8,128)} %shard_map.100) | data formatting | bytes 1048576

commit v3 on v2

--- a/solution.py
+++ b/solution.py
@@ -58,9 +58,13 @@
     sent_ref,
     recv_ref,
     perm_ref,
+    perm_t_ref,
+    block_ref,
     moved_ref,
-    picked_ref,
-    dest_hot_ref,
+    source_ref,
+    own_hot_ref,
+    far_ref,
+    near_ref,
     mass_t_ref,
     gath_t_ref,
     out_t_ref,
@@ -74,7 +78,6 @@
     tets = zone_ref.shape[1]
     slots = list_ref.shape[1]
     cap = slots // PARTNERS
-    rows = zones + slots
 
     pairs = (
         (bnew_hbm, bnew_ref),
@@ -109,29 +112,32 @@
 
     r, c = iotas((width, width))
     perm_ref[...] = one_hot(r == (c % nb) * nf + c // nb)
+    perm_t_ref[...] = one_hot(c == (r % nb) * nf + r // nb)
     perm = perm_ref[...]
 
     for load in loads[:8]:
         load.wait()
-    coeff = nn(old_ref[...], perm).astype(BF)
+    coeff = nt(perm_t_ref[...], old_ref[...]).astype(BF)
     quad = 4 * nb
     r, c = iotas((nb, quad))
-    bnew4 = nn(bnew_ref[...].reshape(tables * quads, nb), one_hot(r == c % nb)).astype(BF)
+    bold4 = nn(bold_ref[...].reshape(tables * quads, nb), one_hot(r == c % nb)).astype(BF)
     r, c = iotas((nb, nb))
     eye_nb = one_hot(r == c)
     r, c = iotas((quad, quad))
     same = r // nb == c // nb
     for t in range(tables):
-        high, low = halves(nt(eye_nb, bold_ref[t]) * weight_ref[t : t + 1, :])
-        new_t = bnew4[t * quads : (t + 1) * quads]
-        both = nn(high, new_t) + nn(low, new_t)
-        block = jnp.where(same, jnp.concatenate([both] * 4, axis=0), 0.0)
-        block = block.astype(BF)
-        for h in range(width // quad):
-            part = coeff[:, h * quad : (h + 1) * quad]
-            moved_ref[t * zones : (t + 1) * zones, h * quad : (h + 1) * quad] = nn(
-                part, block
-            ).astype(BF)
+        high, low = halves(nt(eye_nb, bnew_ref[t]) * weight_ref[t : t + 1, :])
+        old_t = bold4[t * quads : (t + 1) * quads]
+        both = nn(high, old_t) + nn(low, old_t)
+        block_ref[t * quad : (t + 1) * quad, :] = jnp.where(
+            same, jnp.concatenate([both] * 4, axis=0), 0.0
+        ).astype(BF)
+    for h in range(width // quad):
+        part = nn(block_ref[...], coeff[h * quad : (h + 1) * quad]).astype(BF)
+        for t in range(tables):
+            moved_ref[h * quad : (h + 1) * quad, t * zones : (t + 1) * zones] = part[
+                t * quad : (t + 1) * quad
+            ]
 
     numbers = iotas((zones, tets))[0].astype(F32).astype(BF)
     one, zero = jnp.ones((), BF), jnp.zeros((), BF)
@@ -139,15 +145,21 @@
     dest = dest_ref[...]
     own_zone = jnp.where(dest < zones, dest, -1).astype(F32).astype(BF)
     far_slot = jnp.where(dest < zones, -1, dest - zones).astype(F32).astype(BF)
-    dest_hot_ref[:zones, :] = jnp.where(own_zone == numbers, volume, zero)
-    dest_hot_ref[zones:, :] = jnp.where(far_slot == numbers[:slots], volume, zero)
-    for t in range(tables):
-        of_table = jnp.where(table_ref[...] == t, zone_ref[...], -1).astype(F32).astype(BF)
-        picked_ref[:, t * zones : (t + 1) * zones] = nt(
-            dest_hot_ref[...], jnp.where(of_table == numbers, one, zero)
-        ).astype(BF)
-
-    sent_ref[...] = nn(picked_ref[zones:, :], moved_ref[...]).astype(BF)
+    far_hot = jnp.where(far_slot == numbers[:slots], volume, zero)
+    own_hot_ref[...] = jnp.where(own_zone == numbers, volume, zero)
+    chunk = 2
+    for t0 in range(0, tables, chunk):
+        for t in range(t0, t0 + chunk):
+            of_table = jnp.where(table_ref[...] == t, zone_ref[...], -1)
+            source_ref[t * zones : (t + 1) * zones, :] = jnp.where(
+                of_table.astype(F32).astype(BF) == numbers, one, zero
+            )
+        at = slice(t0 * zones, (t0 + chunk) * zones)
+        far_ref[at, :] = nt(source_ref[at, :], far_hot).astype(BF)
+
+    far_t = nn(moved_ref[...], far_ref[...]).astype(BF)
+    r, c = iotas((slots, slots))
+    sent_ref[...] = nt(one_hot(r == c), far_t).astype(BF)
     pl.semaphore_wait(barrier, PARTNERS)
     copies = []
     for k, where in enumerate(partners):
@@ -162,7 +174,8 @@
         copy.start()
         copies.append(copy)
 
-    own = nn(picked_ref[:zones, :], moved_ref[...])
+    near_ref[...] = nt(source_ref[...], own_hot_ref[...]).astype(BF)
+    gath_t_ref[...] = nn(moved_ref[...], near_ref[...])
     loads[9].wait()
     for o in range(nb // nf):
         mass_t_ref[o * width : (o + 1) * width, :] = nt(
@@ -174,31 +187,33 @@
 
     for copy in copies:
         copy.wait()
-    gathered = own + nn(list_hot, recv_ref[...])
-    high, low = halves(gathered)
-    gath_t_ref[...] = nt(perm, high) + nt(perm, low)
+    gath_t_ref[...] += lax.dot_general(
+        recv_ref[...], list_hot, (((0,), (1,)), ((), ())), preferred_element_type=F32
+    )
 
     lanes = 128
     group = 4
     octets = nb // nf
-    per_step = 4
     for h in range(zones // lanes):
         at = slice(h * lanes, (h + 1) * lanes)
         for f0 in range(0, nf, group):
 
             def step(i, sums):
                 sums = list(sums)
-                for u in range(per_step):
-                    base = pl.multiple_of((i * per_step + u) * nf, nf)
-                    column = gath_t_ref[pl.ds(base, nf), at]
+                base = pl.multiple_of(i * nf, nf)
+                columns = [
+                    gath_t_ref[pl.ds((f0 + f) * nb + base, nf), at] for f in range(group)
+                ]
+                for u in range(nf):
+                    row = pl.multiple_of((i * nf + u) * nf, nf)
                     for o in range(octets):
-                        mass = mass_t_ref[pl.ds(o * width + base, nf), at]
+                        mass = mass_t_ref[pl.ds(o * width + row, nf), at]
                         for f in range(group):
-                            sums[o * group + f] += mass * column[f0 + f : f0 + f + 1, :]
+                            sums[o * group + f] += mass * columns[f][u : u + 1, :]
                 return tuple(sums)
 
             start = tuple(jnp.zeros((nf, lanes), F32) for _ in range(octets * group))
-            sums = lax.fori_loop(0, nb // per_step, step, start)
+            sums = lax.fori_loop(0, nb // nf, step, start)
             for o in range(octets):
                 for f in range(group):
                     out_t_ref[h, pl.ds(o * nf * nf + f0 + f, nf, stride=nf), :] = sums[
@@ -229,7 +244,6 @@
     nb = basis_old.shape[2]
     tets = tet_zone.shape[0]
     slots = recv_list.shape[1]
-    rows = zones + slots
     operands = (
         old_coeff,
         basis_old,
@@ -252,9 +266,13 @@
             pltpu.VMEM((slots, width), BF),
             pltpu.VMEM((slots, width), BF),
             pltpu.VMEM((width, width), BF),
-            pltpu.VMEM((tables * zones, width), BF),
-            pltpu.VMEM((rows, tables * zones), BF),
-            pltpu.VMEM((rows, tets), BF),
+            pltpu.VMEM((width, width), BF),
+            pltpu.VMEM((tables * 4 * nb, 4 * nb), BF),
+            pltpu.VMEM((width, tables * zones), BF),
+            pltpu.VMEM((tables * zones, tets), BF),
+            pltpu.VMEM((zones, tets), BF),
+            pltpu.VMEM((tables * zones, slots), BF),
+            pltpu.VMEM((tables * zones, zones), BF),
             pltpu.VMEM((nb * nb, zones), F32),
             pltpu.VMEM((width, zones), F32),
             pltpu.VMEM((zones // 128, width, 128), F32),
@@ -263,9 +281,9 @@
             pltpu.SemaphoreType.DMA((PARTNERS,)),
         ],
         compiler_params=pltpu.CompilerParams(
-            collective_id=0, has_side_effects=True, vmem_limit_bytes=62 * 2**20
+            collective_id=0, has_side_effects=True, vmem_limit_bytes=52 * 2**20
         ),
-    )(*operands)
+    )(*(pltpu.with_memory_space_constraint(x, pltpu.HBM) for x in operands))
 
 
 def solution(mesh):

time: 24 us -> 23.8 us (level)
  local copies, waits for them, and re-layouts: 1.87 us -> 0.8 us
  Pallas kernels: 22 us -> 22.8 us
    unnamed x1, local copies, waits for them, and re-layouts: 1.87 us -> 0.8 us
    pallas_call x1, Pallas kernels: 22 us -> 22.8 us  [on_device(): pl.pallas_call(kernel, out_shape=jax.ShapeDtypeStruct((zones, width), F32...]
where the time goes in v3:
time: 23.8 us; the launch traced here: 23.6 us
  Pallas kernels  22.8 us (96%)
  local copies, waits for them, and re-layouts  0.8 us (3%)
    pallas_call x1, Pallas kernels, on_device(): pl.pallas_call(kernel, out_shape=jax.ShapeDtypeStruct((zones, width), F32...  22.8 us
    unnamed x1, local copies, waits for them, and re-layouts  0.8 us

profile of v3, /device:TPU:1, one launch (start us, length us, event | category | flops | bytes accessed | tf_op | source)
XLA Modules:
  0.0 23.6 jit_solution(10650262129375776644)
XLA Ops:
  0.0 22.8 %shard_map.100 = f32[256,512]{1,0:T(8,128)S(1)} custom-call(bf16[256,512]{1,0:T(8,128)(2,1)} %old_hbm.1, bf16[8,64,64]{2,1,0:T(8,128)(2,1)} %bold_hbm.1, bf16[8,64,64]{2,1,0:T(8,128)(2,1)} %bnew_hbm.1, f32[8,64]{1,0:T(8,128)} %weight_hbm.1, s32[1,2048]{1,0:T(1,128)} %bitcast.4, s32[1,2048]{1,0:T(1,128)} %bitcast.5, f32[1,2048]{1,0:T(1,128)} %bitcast.6, ...), custom_call_target="tpu_custom_call" | custom-call | tf_op jit(solution)/shard_map/pallas_call | solution.py:259
  22.8 0.8 %copy.12 = f32[256,512]{1,0:T(8,128)} copy(f32[256,512]{1,0:T(8,128)S(1)} %shard_map.100) | data formatting | bytes 1048576

commit v4 on v2

--- a/solution.py
+++ b/solution.py
@@ -59,8 +59,11 @@
     recv_ref,
     perm_ref,
     moved_ref,
-    picked_ref,
-    dest_hot_ref,
+    zone_hot_ref,
+    far_hot_ref,
+    own_hot_ref,
+    far_ref,
+    near_ref,
     mass_t_ref,
     gath_t_ref,
     out_t_ref,
@@ -74,7 +77,6 @@
     tets = zone_ref.shape[1]
     slots = list_ref.shape[1]
     cap = slots // PARTNERS
-    rows = zones + slots
 
     pairs = (
         (bnew_hbm, bnew_ref),
@@ -135,19 +137,26 @@
 
     numbers = iotas((zones, tets))[0].astype(F32).astype(BF)
     one, zero = jnp.ones((), BF), jnp.zeros((), BF)
+    zone_hot_ref[...] = jnp.where(zone_ref[...].astype(F32).astype(BF) == numbers, one, zero)
     volume = volume_ref[...].astype(BF)
-    dest = dest_ref[...]
-    own_zone = jnp.where(dest < zones, dest, -1).astype(F32).astype(BF)
-    far_slot = jnp.where(dest < zones, -1, dest - zones).astype(F32).astype(BF)
-    dest_hot_ref[:zones, :] = jnp.where(own_zone == numbers, volume, zero)
-    dest_hot_ref[zones:, :] = jnp.where(far_slot == numbers[:slots], volume, zero)
-    for t in range(tables):
-        of_table = jnp.where(table_ref[...] == t, zone_ref[...], -1).astype(F32).astype(BF)
-        picked_ref[:, t * zones : (t + 1) * zones] = nt(
-            dest_hot_ref[...], jnp.where(of_table == numbers, one, zero)
-        ).astype(BF)
-
-    sent_ref[...] = nn(picked_ref[zones:, :], moved_ref[...]).astype(BF)
+
+    def spread(target_ref, count, first):
+        for t in range(tables):
+            wanted = (table_ref[...] == t) & (dest_ref[...] >= first)
+            wanted &= dest_ref[...] < first + count
+            row = jnp.where(wanted, dest_ref[...] - first, -1).astype(F32).astype(BF)
+            target_ref[t * count : (t + 1) * count, :] = jnp.where(
+                row == numbers[:count], volume, zero
+            )
+
+    def summed(target_ref, sums_ref, count):
+        sums = nt(target_ref[...], zone_hot_ref[...]).astype(BF)
+        for t in range(tables):
+            sums_ref[:, t * zones : (t + 1) * zones] = sums[t * count : (t + 1) * count]
+        return nn(sums_ref[...], moved_ref[...])
+
+    spread(far_hot_ref, slots, zones)
+    sent_ref[...] = summed(far_hot_ref, far_ref, slots).astype(BF)
     pl.semaphore_wait(barrier, PARTNERS)
     copies = []
     for k, where in enumerate(partners):
@@ -162,48 +171,57 @@
         copy.start()
         copies.append(copy)
 
-    own = nn(picked_ref[:zones, :], moved_ref[...])
+    spread(own_hot_ref, zones, 0)
+    own = summed(own_hot_ref, near_ref, zones)
+    r, c = iotas((zones, zones))
+    eye = one_hot(r == c)
+    high, low = halves(own)
+    for at in range(0, width, zones):
+        part = slice(at, at + zones)
+        gath_t_ref[part, :] = nt(eye, high[:, part]) + nt(eye, low[:, part])
     loads[9].wait()
-    for o in range(nb // nf):
-        mass_t_ref[o * width : (o + 1) * width, :] = nt(
-            perm, mass_ref[:, o * width : (o + 1) * width]
-        )
+    for at in range(0, nb * nb, zones):
+        part = slice(at, at + zones)
+        mass_t_ref[part, :] = nt(eye, mass_ref[:, part])
     loads[8].wait()
     r, _ = iotas((zones, slots))
     list_hot = one_hot(list_ref[...] == r)
 
     for copy in copies:
         copy.wait()
-    gathered = own + nn(list_hot, recv_ref[...])
-    high, low = halves(gathered)
-    gath_t_ref[...] = nt(perm, high) + nt(perm, low)
+    for at in range(0, width, zones):
+        part = slice(at, at + zones)
+        recv_t = nt(eye, recv_ref[:, part]).astype(BF)
+        gath_t_ref[part, :] += nt(recv_t, list_hot)
 
     lanes = 128
     group = 4
-    octets = nb // nf
-    per_step = 4
+    octet = 8
     for h in range(zones // lanes):
         at = slice(h * lanes, (h + 1) * lanes)
         for f0 in range(0, nf, group):
 
-            def step(i, sums):
-                sums = list(sums)
-                for u in range(per_step):
-                    base = pl.multiple_of((i * per_step + u) * nf, nf)
-                    column = gath_t_ref[pl.ds(base, nf), at]
-                    for o in range(octets):
-                        mass = mass_t_ref[pl.ds(o * width + base, nf), at]
-                        for f in range(group):
-                            sums[o * group + f] += mass * column[f0 + f : f0 + f + 1, :]
-                return tuple(sums)
-
-            start = tuple(jnp.zeros((nf, lanes), F32) for _ in range(octets * group))
-            sums = lax.fori_loop(0, nb // per_step, step, start)
-            for o in range(octets):
-                for f in range(group):
-                    out_t_ref[h, pl.ds(o * nf * nf + f0 + f, nf, stride=nf), :] = sums[
-                        o * group + f
+            def step(i, carry):
+                columns = [
+                    [gath_t_ref[pl.ds(f * nb + k, octet), at] for k in range(0, nb, octet)]
+                    for f in range(f0, f0 + group)
+                ]
+                for u in range(octet):
+                    j = i * octet + u
+                    mass = [
+                        mass_t_ref[pl.ds(pl.multiple_of(j * nb + k, octet), octet), at]
+                        for k in range(0, nb, octet)
                     ]
+                    for f in range(group):
+                        terms = [m * g for m, g in zip(mass, columns[f])]
+                        while len(terms) > 1:
+                            terms = [x + y for x, y in zip(terms[::2], terms[1::2])]
+                        out_t_ref[h, pl.ds(j * nf + f0 + f, 1), :] = jnp.sum(
+                            terms[0], axis=0, keepdims=True
+                        )
+                return carry
+
+            lax.fori_loop(0, nb // octet, step, 0)
 
     r, c = iotas((lanes, lanes))
     eye = one_hot(r == c)
@@ -229,7 +247,6 @@
     nb = basis_old.shape[2]
     tets = tet_zone.shape[0]
     slots = recv_list.shape[1]
-    rows = zones + slots
     operands = (
         old_coeff,
         basis_old,
@@ -253,8 +270,11 @@
             pltpu.VMEM((slots, width), BF),
             pltpu.VMEM((width, width), BF),
             pltpu.VMEM((tables * zones, width), BF),
-            pltpu.VMEM((rows, tables * zones), BF),
-            pltpu.VMEM((rows, tets), BF),
+            pltpu.VMEM((zones, tets), BF),
+            pltpu.VMEM((tables * slots, tets), BF),
+            pltpu.VMEM((tables * zones, tets), BF),
+            pltpu.VMEM((slots, tables * zones), BF),
+            pltpu.VMEM((zones, tables * zones), BF),
             pltpu.VMEM((nb * nb, zones), F32),
             pltpu.VMEM((width, zones), F32),
             pltpu.VMEM((zones // 128, width, 128), F32),
@@ -263,9 +283,9 @@
             pltpu.SemaphoreType.DMA((PARTNERS,)),
         ],
         compiler_params=pltpu.CompilerParams(
-            collective_id=0, has_side_effects=True, vmem_limit_bytes=62 * 2**20
+            collective_id=0, has_side_effects=True, vmem_limit_bytes=52 * 2**20
         ),
-    )(*operands)
+    )(*(pltpu.with_memory_space_constraint(x, pltpu.HBM) for x in operands))
 
 
 def solution(mesh):

time: 24 us -> 20.8 us (0.87)
  Pallas kernels: 22 us -> 19.9 us
  local copies, waits for them, and re-layouts: 1.87 us -> 0.8 us
    pallas_call x1, Pallas kernels: 22 us -> 19.9 us  [on_device(): pl.pallas_call(kernel, out_shape=jax.ShapeDtypeStruct((zones, width), F32...]
    unnamed x1, local copies, waits for them, and re-layouts: 1.87 us -> 0.8 us
where the time goes in v4:
time: 20.8 us; the launch traced here: 20.7 us
  Pallas kernels  19.9 us (96%)
  local copies, waits for them, and re-layouts  0.8 us (4%)
    pallas_call x1, Pallas kernels, on_device(): pl.pallas_call(kernel, out_shape=jax.ShapeDtypeStruct((zones, width), F32...  19.9 us
    unnamed x1, local copies, waits for them, and re-layouts  0.8 us

profile of v4, /device:TPU:1, one launch (start us, length us, event | category | flops | bytes accessed | tf_op | source)
XLA Modules:
  0.0 20.7 jit_solution(9190043952419556816)
XLA Ops:
  0.0 19.9 %shard_map.100 = f32[256,512]{1,0:T(8,128)S(1)} custom-call(bf16[256,512]{1,0:T(8,128)(2,1)} %old_hbm.1, bf16[8,64,64]{2,1,0:T(8,128)(2,1)} %bold_hbm.1, bf16[8,64,64]{2,1,0:T(8,128)(2,1)} %bnew_hbm.1, f32[8,64]{1,0:T(8,128)} %weight_hbm.1, s32[1,2048]{1,0:T(1,128)} %bitcast.4, s32[1,2048]{1,0:T(1,128)} %bitcast.5, f32[1,2048]{1,0:T(1,128)} %bitcast.6, ...), custom_call_target="tpu_custom_call" | custom-call | tf_op jit(solution)/shard_map/pallas_call | solution.py:262
  19.9 0.8 %copy.12 = f32[256,512]{1,0:T(8,128)} copy(f32[256,512]{1,0:T(8,128)S(1)} %shard_map.100) | data formatting | bytes 1048576

commit v5 on v4

--- a/solution.py
+++ b/solution.py
@@ -79,13 +79,13 @@
     cap = slots // PARTNERS
 
     pairs = (
+        (zone_hbm, zone_ref),
+        (table_hbm, table_ref),
+        (dest_hbm, dest_ref),
+        (volume_hbm, volume_ref),
         (bnew_hbm, bnew_ref),
         (bold_hbm, bold_ref),
         (weight_hbm, weight_ref),
-        (dest_hbm, dest_ref),
-        (volume_hbm, volume_ref),
-        (zone_hbm, zone_ref),
-        (table_hbm, table_ref),
         (old_hbm, old_ref),
         (list_hbm, list_ref),
         (mass_hbm, mass_ref),
@@ -113,7 +113,32 @@
     perm_ref[...] = one_hot(r == (c % nb) * nf + c // nb)
     perm = perm_ref[...]
 
-    for load in loads[:8]:
+    for load in loads[:4]:
+        load.wait()
+    numbers = iotas((zones, tets))[0].astype(F32).astype(BF)
+    one, zero = jnp.ones((), BF), jnp.zeros((), BF)
+    zone_hot_ref[...] = jnp.where(zone_ref[...].astype(F32).astype(BF) == numbers, one, zero)
+    volume = volume_ref[...].astype(BF)
+
+    in_table = [
+        jnp.where(table_ref[...] == t, 1.0, 0.0).astype(BF) for t in range(tables)
+    ]
+
+    def summed(target, hot_ref, sums_ref, chunk):
+        count = target.shape[0]
+        for t0 in range(0, tables, chunk):
+            for t in range(t0, t0 + chunk):
+                hot_ref[t * count : (t + 1) * count, :] = target * in_table[t]
+            part = hot_ref[t0 * count : (t0 + chunk) * count, :]
+            sums = nt(part, zone_hot_ref[...]).astype(BF)
+            for t in range(chunk):
+                at = (t0 + t) * zones
+                sums_ref[:, at : at + zones] = sums[t * count : (t + 1) * count]
+
+    dest = dest_ref[...]
+    far_slot = jnp.where(dest < zones, -1, dest - zones).astype(F32).astype(BF)
+    summed(jnp.where(far_slot == numbers[:slots], volume, zero), far_hot_ref, far_ref, 4)
+    for load in loads[4:8]:
         load.wait()
     coeff = nn(old_ref[...], perm).astype(BF)
     quad = 4 * nb
@@ -135,28 +160,7 @@
                 part, block
             ).astype(BF)
 
-    numbers = iotas((zones, tets))[0].astype(F32).astype(BF)
-    one, zero = jnp.ones((), BF), jnp.zeros((), BF)
-    zone_hot_ref[...] = jnp.where(zone_ref[...].astype(F32).astype(BF) == numbers, one, zero)
-    volume = volume_ref[...].astype(BF)
-
-    def spread(target_ref, count, first):
-        for t in range(tables):
-            wanted = (table_ref[...] == t) & (dest_ref[...] >= first)
-            wanted &= dest_ref[...] < first + count
-            row = jnp.where(wanted, dest_ref[...] - first, -1).astype(F32).astype(BF)
-            target_ref[t * count : (t + 1) * count, :] = jnp.where(
-                row == numbers[:count], volume, zero
-            )
-
-    def summed(target_ref, sums_ref, count):
-        sums = nt(target_ref[...], zone_hot_ref[...]).astype(BF)
-        for t in range(tables):
-            sums_ref[:, t * zones : (t + 1) * zones] = sums[t * count : (t + 1) * count]
-        return nn(sums_ref[...], moved_ref[...])
-
-    spread(far_hot_ref, slots, zones)
-    sent_ref[...] = summed(far_hot_ref, far_ref, slots).astype(BF)
+    sent_ref[...] = nn(far_ref[...], moved_ref[...]).astype(BF)
     pl.semaphore_wait(barrier, PARTNERS)
     copies = []
     for k, where in enumerate(partners):
@@ -171,8 +175,9 @@
         copy.start()
         copies.append(copy)
 
-    spread(own_hot_ref, zones, 0)
-    own = summed(own_hot_ref, near_ref, zones)
+    own_zone = jnp.where(dest < zones, dest, -1).astype(F32).astype(BF)
+    summed(jnp.where(own_zone == numbers, volume, zero), own_hot_ref, near_ref, 2)
+    own = nn(near_ref[...], moved_ref[...])
     r, c = iotas((zones, zones))
     eye = one_hot(r == c)
     high, low = halves(own)
@@ -195,33 +200,53 @@
         gath_t_ref[part, :] += nt(recv_t, list_hot)
 
     lanes = 128
-    group = 4
+    group = 2
     octet = 8
+    row, _ = iotas((octet, lanes))
+
+    def folded(sums):
+        shift = octet // 2
+        while shift:
+            first = (row & shift) == 0
+            paired = []
+            for x, y in zip(sums[:shift], sums[shift:]):
+                if shift == octet // 2:
+                    other = pltpu.roll(jnp.where(first, y, x), shift, 0)
+                    paired.append(jnp.where(first, x, y) + other)
+                else:
+                    x = x + pltpu.roll(x, octet - shift, 0)
+                    y = y + pltpu.roll(y, shift, 0)
+                    paired.append(jnp.where(first, x, y))
+            sums = paired
+            shift //= 2
+        return sums[0]
+
     for h in range(zones // lanes):
         at = slice(h * lanes, (h + 1) * lanes)
-        for f0 in range(0, nf, group):
-
-            def step(i, carry):
+
+        def step(i, carry):
+            for f0 in range(0, nf, group):
                 columns = [
                     [gath_t_ref[pl.ds(f * nb + k, octet), at] for k in range(0, nb, octet)]
                     for f in range(f0, f0 + group)
                 ]
+                sums = [[] for _ in range(group)]
                 for u in range(octet):
-                    j = i * octet + u
+                    base = pl.multiple_of((i * octet + u) * nb, octet)
                     mass = [
-                        mass_t_ref[pl.ds(pl.multiple_of(j * nb + k, octet), octet), at]
-                        for k in range(0, nb, octet)
+                        mass_t_ref[pl.ds(base + k, octet), at] for k in range(0, nb, octet)
                     ]
                     for f in range(group):
                         terms = [m * g for m, g in zip(mass, columns[f])]
                         while len(terms) > 1:
                             terms = [x + y for x, y in zip(terms[::2], terms[1::2])]
-                        out_t_ref[h, pl.ds(j * nf + f0 + f, 1), :] = jnp.sum(
-                            terms[0], axis=0, keepdims=True
-                        )
-                return carry
-
-            lax.fori_loop(0, nb // octet, step, 0)
+                        sums[f].append(terms[0])
+                for f in range(group):
+                    place = pl.ds(i * octet * nf + f0 + f, octet, stride=nf)
+                    out_t_ref[h, place, :] = folded(sums[f])
+            return carry
+
+        lax.fori_loop(0, nb // octet, step, 0)
 
     r, c = iotas((lanes, lanes))
     eye = one_hot(r == c)

time: 20.8 us -> 23 us (1.11)
  Pallas kernels: 19.9 us -> 22 us
    pallas_call x1, Pallas kernels: 19.9 us -> 22 us  [on_device(): pl.pallas_call(kernel, out_shape=jax.ShapeDtypeStruct((zones, width), F32...]
where the time goes in v5:
time: 23 us; the launch traced here: 22.8 us
  Pallas kernels  22 us (96%)
  local copies, waits for them, and re-layouts  0.8 us (3%)
    pallas_call x1, Pallas kernels, on_device(): pl.pallas_call(kernel, out_shape=jax.ShapeDtypeStruct((zones, width), F32...  22 us
    unnamed x1, local copies, waits for them, and re-layouts  0.8 us

profile of v5, /device:TPU:1, one launch (start us, length us, event | category | flops | bytes accessed | tf_op | source)
XLA Modules:
  0.0 22.8 jit_solution(2976630600707902244)
XLA Ops:
  0.0 22.0 %shard_map.100 = f32[256,512]{1,0:T(8,128)S(1)} custom-call(bf16[256,512]{1,0:T(8,128)(2,1)} %old_hbm.1, bf16[8,64,64]{2,1,0:T(8,128)(2,1)} %bold_hbm.1, bf16[8,64,64]{2,1,0:T(8,128)(2,1)} %bnew_hbm.1, f32[8,64]{1,0:T(8,128)} %weight_hbm.1, s32[1,2048]{1,0:T(1,128)} %bitcast.4, s32[1,2048]{1,0:T(1,128)} %bitcast.5, f32[1,2048]{1,0:T(1,128)} %bitcast.6, ...), custom_call_target="tpu_custom_call" | custom-call | tf_op jit(solution)/shard_map/pallas_call | solution.py:287
  22.0 0.8 %copy.12 = f32[256,512]{1,0:T(8,128)} copy(f32[256,512]{1,0:T(8,128)S(1)} %shard_map.100) | data formatting | bytes 1048576

commit v6 on v5

--- a/solution.py
+++ b/solution.py
@@ -94,7 +94,7 @@
         pltpu.make_async_copy(source, target, in_sem.at[i])
         for i, (source, target) in enumerate(pairs)
     ]
-    for load in loads:
+    for load in loads[:9]:
         load.start()
 
     a, b = lax.axis_index("gx"), lax.axis_index("yz")
@@ -113,33 +113,9 @@
     perm_ref[...] = one_hot(r == (c % nb) * nf + c // nb)
     perm = perm_ref[...]
 
-    for load in loads[:4]:
+    for load in loads[:8]:
         load.wait()
-    numbers = iotas((zones, tets))[0].astype(F32).astype(BF)
-    one, zero = jnp.ones((), BF), jnp.zeros((), BF)
-    zone_hot_ref[...] = jnp.where(zone_ref[...].astype(F32).astype(BF) == numbers, one, zero)
-    volume = volume_ref[...].astype(BF)
-
-    in_table = [
-        jnp.where(table_ref[...] == t, 1.0, 0.0).astype(BF) for t in range(tables)
-    ]
-
-    def summed(target, hot_ref, sums_ref, chunk):
-        count = target.shape[0]
-        for t0 in range(0, tables, chunk):
-            for t in range(t0, t0 + chunk):
-                hot_ref[t * count : (t + 1) * count, :] = target * in_table[t]
-            part = hot_ref[t0 * count : (t0 + chunk) * count, :]
-            sums = nt(part, zone_hot_ref[...]).astype(BF)
-            for t in range(chunk):
-                at = (t0 + t) * zones
-                sums_ref[:, at : at + zones] = sums[t * count : (t + 1) * count]
-
-    dest = dest_ref[...]
-    far_slot = jnp.where(dest < zones, -1, dest - zones).astype(F32).astype(BF)
-    summed(jnp.where(far_slot == numbers[:slots], volume, zero), far_hot_ref, far_ref, 4)
-    for load in loads[4:8]:
-        load.wait()
+    loads[9].start()
     coeff = nn(old_ref[...], perm).astype(BF)
     quad = 4 * nb
     r, c = iotas((nb, quad))
@@ -160,6 +136,29 @@
                 part, block
             ).astype(BF)
 
+    numbers = iotas((zones, tets))[0].astype(F32).astype(BF)
+    one, zero = jnp.ones((), BF), jnp.zeros((), BF)
+    zone_hot_ref[...] = jnp.where(zone_ref[...].astype(F32).astype(BF) == numbers, one, zero)
+    volume = volume_ref[...].astype(BF)
+
+    in_table = [
+        jnp.where(table_ref[...] == t, 1.0, 0.0).astype(BF) for t in range(tables)
+    ]
+
+    def summed(target, hot_ref, sums_ref, chunk):
+        count = target.shape[0]
+        for t0 in range(0, tables, chunk):
+            for t in range(t0, t0 + chunk):
+                hot_ref[t * count : (t + 1) * count, :] = target * in_table[t]
+            part = hot_ref[t0 * count : (t0 + chunk) * count, :]
+            sums = nt(part, zone_hot_ref[...]).astype(BF)
+            for t in range(chunk):
+                at = (t0 + t) * zones
+                sums_ref[:, at : at + zones] = sums[t * count : (t + 1) * count]
+
+    dest = dest_ref[...]
+    far_slot = jnp.where(dest < zones, -1, dest - zones).astype(F32).astype(BF)
+    summed(jnp.where(far_slot == numbers[:slots], volume, zero), far_hot_ref, far_ref, tables)
     sent_ref[...] = nn(far_ref[...], moved_ref[...]).astype(BF)
     pl.semaphore_wait(barrier, PARTNERS)
     copies = []

time: 23 us -> 25.7 us (1.12)
  Pallas kernels: 22 us -> 24.7 us
    pallas_call x1, Pallas kernels: 22 us -> 24.7 us  [on_device(): pl.pallas_call(kernel, out_shape=jax.ShapeDtypeStruct((zones, width), F32...]
where the time goes in v6:
time: 25.7 us; the launch traced here: 25.5 us
  Pallas kernels  24.7 us (96%)
  local copies, waits for them, and re-layouts  0.8 us (3%)
    pallas_call x1, Pallas kernels, on_device(): pl.pallas_call(kernel, out_shape=jax.ShapeDtypeStruct((zones, width), F32...  24.7 us
    unnamed x1, local copies, waits for them, and re-layouts  0.8 us

profile of v6, /device:TPU:1, one launch (start us, length us, event | category | flops | bytes accessed | tf_op | source)
XLA Modules:
  0.0 25.5 jit_solution(13205486471156168946)
XLA Ops:
  0.0 24.7 %shard_map.100 = f32[256,512]{1,0:T(8,128)S(1)} custom-call(bf16[256,512]{1,0:T(8,128)(2,1)} %old_hbm.1, bf16[8,64,64]{2,1,0:T(8,128)(2,1)} %bold_hbm.1, bf16[8,64,64]{2,1,0:T(8,128)(2,1)} %bnew_hbm.1, f32[8,64]{1,0:T(8,128)} %weight_hbm.1, s32[1,2048]{1,0:T(1,128)} %bitcast.4, s32[1,2048]{1,0:T(1,128)} %bitcast.5, f32[1,2048]{1,0:T(1,128)} %bitcast.6, ...), custom_call_target="tpu_custom_call" | custom-call | tf_op jit(solution)/shard_map/pallas_call | solution.py:286
  24.7 0.8 %copy.12 = f32[256,512]{1,0:T(8,128)} copy(f32[256,512]{1,0:T(8,128)S(1)} %shard_map.100) | data formatting | bytes 1048576

commit v7 on v4

--- a/solution.py
+++ b/solution.py
@@ -171,8 +171,20 @@
         copy.start()
         copies.append(copy)
 
-    spread(own_hot_ref, zones, 0)
-    own = summed(own_hot_ref, near_ref, zones)
+    own_zone = jnp.where(dest_ref[...] < zones, dest_ref[...], -1).astype(F32).astype(BF)
+    own_hot = jnp.where(own_zone == numbers, volume, zero)
+    chunk = 2
+    for t0 in range(0, tables, chunk):
+        for t in range(t0, t0 + chunk):
+            own_hot_ref[t * zones : (t + 1) * zones, :] = own_hot * jnp.where(
+                table_ref[...] == t, 1.0, 0.0
+            ).astype(BF)
+        part = own_hot_ref[t0 * zones : (t0 + chunk) * zones, :]
+        sums = nt(part, zone_hot_ref[...]).astype(BF)
+        for t in range(chunk):
+            at = (t0 + t) * zones
+            near_ref[:, at : at + zones] = sums[t * zones : (t + 1) * zones]
+    own = nn(near_ref[...], moved_ref[...])
     r, c = iotas((zones, zones))
     eye = one_hot(r == c)
     high, low = halves(own)
@@ -195,33 +207,53 @@
         gath_t_ref[part, :] += nt(recv_t, list_hot)
 
     lanes = 128
-    group = 4
+    group = 2
     octet = 8
+    row, _ = iotas((octet, lanes))
+
+    def folded(sums):
+        shift = octet // 2
+        while shift:
+            first = (row & shift) == 0
+            paired = []
+            for x, y in zip(sums[:shift], sums[shift:]):
+                if shift == octet // 2:
+                    other = pltpu.roll(jnp.where(first, y, x), shift, 0)
+                    paired.append(jnp.where(first, x, y) + other)
+                else:
+                    x = x + pltpu.roll(x, octet - shift, 0)
+                    y = y + pltpu.roll(y, shift, 0)
+                    paired.append(jnp.where(first, x, y))
+            sums = paired
+            shift //= 2
+        return sums[0]
+
     for h in range(zones // lanes):
         at = slice(h * lanes, (h + 1) * lanes)
-        for f0 in range(0, nf, group):
-
-            def step(i, carry):
+
+        def step(i, carry):
+            for f0 in range(0, nf, group):
                 columns = [
                     [gath_t_ref[pl.ds(f * nb + k, octet), at] for k in range(0, nb, octet)]
                     for f in range(f0, f0 + group)
                 ]
+                sums = [[] for _ in range(group)]
                 for u in range(octet):
-                    j = i * octet + u
+                    base = pl.multiple_of((i * octet + u) * nb, octet)
                     mass = [
-                        mass_t_ref[pl.ds(pl.multiple_of(j * nb + k, octet), octet), at]
-                        for k in range(0, nb, octet)
+                        mass_t_ref[pl.ds(base + k, octet), at] for k in range(0, nb, octet)
                     ]
                     for f in range(group):
                         terms = [m * g for m, g in zip(mass, columns[f])]
                         while len(terms) > 1:
                             terms = [x + y for x, y in zip(terms[::2], terms[1::2])]
-                        out_t_ref[h, pl.ds(j * nf + f0 + f, 1), :] = jnp.sum(
-                            terms[0], axis=0, keepdims=True
-                        )
-                return carry
-
-            lax.fori_loop(0, nb // octet, step, 0)
+                        sums[f].append(terms[0])
+                for f in range(group):
+                    place = pl.ds(i * octet * nf + f0 + f, octet, stride=nf)
+                    out_t_ref[h, place, :] = folded(sums[f])
+            return carry
+
+        lax.fori_loop(0, nb // octet, step, 0)
 
     r, c = iotas((lanes, lanes))
     eye = one_hot(r == c)

time: 20.8 us -> 21.7 us (1.043)
  Pallas kernels: 19.9 us -> 20.8 us
    pallas_call x1, Pallas kernels: 19.9 us -> 20.8 us  [on_device(): pl.pallas_call(kernel, out_shape=jax.ShapeDtypeStruct((zones, width), F32...]
where the time goes in v7:
time: 21.7 us; the launch traced here: 21.6 us
  Pallas kernels  20.8 us (96%)
  local copies, waits for them, and re-layouts  0.8 us (4%)
    pallas_call x1, Pallas kernels, on_device(): pl.pallas_call(kernel, out_shape=jax.ShapeDtypeStruct((zones, width), F32...  20.8 us
    unnamed x1, local copies, waits for them, and re-layouts  0.8 us

profile of v7, /device:TPU:1, one launch (start us, length us, event | category | flops | bytes accessed | tf_op | source)
XLA Modules:
  0.0 21.6 jit_solution(9519240464506309873)
XLA Ops:
  0.0 20.8 %shard_map.100 = f32[256,512]{1,0:T(8,128)S(1)} custom-call(bf16[256,512]{1,0:T(8,128)(2,1)} %old_hbm.1, bf16[8,64,64]{2,1,0:T(8,128)(2,1)} %bold_hbm.1, bf16[8,64,64]{2,1,0:T(8,128)(2,1)} %bnew_hbm.1, f32[8,64]{1,0:T(8,128)} %weight_hbm.1, s32[1,2048]{1,0:T(1,128)} %bitcast.4, s32[1,2048]{1,0:T(1,128)} %bitcast.5, f32[1,2048]{1,0:T(1,128)} %bitcast.6, ...), custom_call_target="tpu_custom_call" | custom-call | tf_op jit(solution)/shard_map/pallas_call | solution.py:294
  20.8 0.8 %copy.12 = f32[256,512]{1,0:T(8,128)} copy(f32[256,512]{1,0:T(8,128)S(1)} %shard_map.100) | data formatting | bytes 1048576

commit v8 on v2

--- a/solution.py
+++ b/solution.py
@@ -59,8 +59,11 @@
     recv_ref,
     perm_ref,
     moved_ref,
-    picked_ref,
-    dest_hot_ref,
+    zone_hot_ref,
+    far_hot_ref,
+    own_hot_ref,
+    far_ref,
+    near_ref,
     mass_t_ref,
     gath_t_ref,
     out_t_ref,
@@ -74,7 +77,6 @@
     tets = zone_ref.shape[1]
     slots = list_ref.shape[1]
     cap = slots // PARTNERS
-    rows = zones + slots
 
     pairs = (
         (bnew_hbm, bnew_ref),
@@ -135,19 +137,26 @@
 
     numbers = iotas((zones, tets))[0].astype(F32).astype(BF)
     one, zero = jnp.ones((), BF), jnp.zeros((), BF)
+    zone_hot_ref[...] = jnp.where(zone_ref[...].astype(F32).astype(BF) == numbers, one, zero)
     volume = volume_ref[...].astype(BF)
-    dest = dest_ref[...]
-    own_zone = jnp.where(dest < zones, dest, -1).astype(F32).astype(BF)
-    far_slot = jnp.where(dest < zones, -1, dest - zones).astype(F32).astype(BF)
-    dest_hot_ref[:zones, :] = jnp.where(own_zone == numbers, volume, zero)
-    dest_hot_ref[zones:, :] = jnp.where(far_slot == numbers[:slots], volume, zero)
-    for t in range(tables):
-        of_table = jnp.where(table_ref[...] == t, zone_ref[...], -1).astype(F32).astype(BF)
-        picked_ref[:, t * zones : (t + 1) * zones] = nt(
-            dest_hot_ref[...], jnp.where(of_table == numbers, one, zero)
-        ).astype(BF)
-
-    sent_ref[...] = nn(picked_ref[zones:, :], moved_ref[...]).astype(BF)
+
+    def spread(target_ref, count, first):
+        for t in range(tables):
+            wanted = (table_ref[...] == t) & (dest_ref[...] >= first)
+            wanted &= dest_ref[...] < first + count
+            row = jnp.where(wanted, dest_ref[...] - first, -1).astype(F32).astype(BF)
+            target_ref[t * count : (t + 1) * count, :] = jnp.where(
+                row == numbers[:count], volume, zero
+            )
+
+    def summed(target_ref, sums_ref, count):
+        sums = nt(target_ref[...], zone_hot_ref[...]).astype(BF)
+        for t in range(tables):
+            sums_ref[:, t * zones : (t + 1) * zones] = sums[t * count : (t + 1) * count]
+        return nn(sums_ref[...], moved_ref[...])
+
+    spread(far_hot_ref, slots, zones)
+    sent_ref[...] = summed(far_hot_ref, far_ref, slots).astype(BF)
     pl.semaphore_wait(barrier, PARTNERS)
     copies = []
     for k, where in enumerate(partners):
@@ -162,7 +171,22 @@
         copy.start()
         copies.append(copy)
 
-    own = nn(picked_ref[:zones, :], moved_ref[...])
+    own_zone = jnp.where(dest_ref[...] < zones, dest_ref[...], -1).astype(F32).astype(BF)
+    own_hot = jnp.where(own_zone == numbers, volume, zero)
+    chunk = 2
+    for t0 in range(0, tables, chunk):
+        for t in range(t0, t0 + chunk):
+            own_hot_ref[t * zones : (t + 1) * zones, :] = own_hot * jnp.where(
+                table_ref[...] == t, 1.0, 0.0
+            ).astype(BF)
+        part = own_hot_ref[t0 * zones : (t0 + chunk) * zones, :]
+        sums = nt(part, zone_hot_ref[...]).astype(BF)
+        for t in range(chunk):
+            at = (t0 + t) * zones
+            near_ref[:, at : at + zones] = sums[t * zones : (t + 1) * zones]
+    own = nn(near_ref[...], moved_ref[...])
+    high, low = halves(own)
+    gath_t_ref[...] = nt(perm, high) + nt(perm, low)
     loads[9].wait()
     for o in range(nb // nf):
         mass_t_ref[o * width : (o + 1) * width, :] = nt(
@@ -174,9 +198,8 @@
 
     for copy in copies:
         copy.wait()
-    gathered = own + nn(list_hot, recv_ref[...])
-    high, low = halves(gathered)
-    gath_t_ref[...] = nt(perm, high) + nt(perm, low)
+    recv_t = nt(perm, recv_ref[...]).astype(BF)
+    gath_t_ref[...] += nt(recv_t, list_hot)
 
     lanes = 128
     group = 4
@@ -229,7 +252,6 @@
     nb = basis_old.shape[2]
     tets = tet_zone.shape[0]
     slots = recv_list.shape[1]
-    rows = zones + slots
     operands = (
         old_coeff,
         basis_old,
@@ -253,8 +275,11 @@
             pltpu.VMEM((slots, width), BF),
             pltpu.VMEM((width, width), BF),
             pltpu.VMEM((tables * zones, width), BF),
-            pltpu.VMEM((rows, tables * zones), BF),
-            pltpu.VMEM((rows, tets), BF),
+            pltpu.VMEM((zones, tets), BF),
+            pltpu.VMEM((tables * slots, tets), BF),
+            pltpu.VMEM((tables * zones, tets), BF),
+            pltpu.VMEM((slots, tables * zones), BF),
+            pltpu.VMEM((zones, tables * zones), BF),
             pltpu.VMEM((nb * nb, zones), F32),
             pltpu.VMEM((width, zones), F32),
             pltpu.VMEM((zones // 128, width, 128), F32),
@@ -263,9 +288,9 @@
             pltpu.SemaphoreType.DMA((PARTNERS,)),
         ],
         compiler_params=pltpu.CompilerParams(
-            collective_id=0, has_side_effects=True, vmem_limit_bytes=62 * 2**20
+            collective_id=0, has_side_effects=True, vmem_limit_bytes=52 * 2**20
         ),
-    )(*operands)
+    )(*(pltpu.with_memory_space_constraint(x, pltpu.HBM) for x in operands))
 
 
 def solution(mesh):

time: 24 us -> 20.6 us (0.86)
  Pallas kernels: 22 us -> 19.7 us
  local copies, waits for them, and re-layouts: 1.87 us -> 0.8 us
    pallas_call x1, Pallas kernels: 22 us -> 19.7 us  [on_device(): pl.pallas_call(kernel, out_shape=jax.ShapeDtypeStruct((zones, width), F32...]
    unnamed x1, local copies, waits for them, and re-layouts: 1.87 us -> 0.8 us
where the time goes in v8:
time: 20.6 us; the launch traced here: 20.5 us
  Pallas kernels  19.7 us (96%)
  local copies, waits for them, and re-layouts  0.8 us (4%)
    pallas_call x1, Pallas kernels, on_device(): pl.pallas_call(kernel, out_shape=jax.ShapeDtypeStruct((zones, width), F32...  19.7 us
    unnamed x1, local copies, waits for them, and re-layouts  0.8 us

profile of v8, /device:TPU:1, one launch (start us, length us, event | category | flops | bytes accessed | tf_op | source)
XLA Modules:
  0.0 20.5 jit_solution(10534960425074728674)
XLA Ops:
  0.0 19.7 %shard_map.100 = f32[256,512]{1,0:T(8,128)S(1)} custom-call(bf16[256,512]{1,0:T(8,128)(2,1)} %old_hbm.1, bf16[8,64,64]{2,1,0:T(8,128)(2,1)} %bold_hbm.1, bf16[8,64,64]{2,1,0:T(8,128)(2,1)} %bnew_hbm.1, f32[8,64]{1,0:T(8,128)} %weight_hbm.1, s32[1,2048]{1,0:T(1,128)} %bitcast.4, s32[1,2048]{1,0:T(1,128)} %bitcast.5, f32[1,2048]{1,0:T(1,128)} %bitcast.6, ...), custom_call_target="tpu_custom_call" | custom-call | tf_op jit(solution)/shard_map/pallas_call | solution.py:267
  19.7 0.8 %copy.12 = f32[256,512]{1,0:T(8,128)} copy(f32[256,512]{1,0:T(8,128)S(1)} %shard_map.100) | data formatting | bytes 1048576
